TPU v7x, 512 devices: a whole 4x4x16 slice. The times are simulated.
512 devices in a mesh: prow: 16 (over z_hi, y, core), pcol: 32 (over x, z_lo).
Axes of the slice: x: 4, y: 4, z: 16 (z_hi: 2, z_lo: 8; z = z_hi * 8 + z_lo), core: 2. Of those that a mesh axis runs over, the one named last changes fastest.
Arguments:
- ainv: bfloat16 [16384, 16384], P('pcol', 'prow'), may hold values from -6 to 6
- lpanel: bfloat16 [16384, 2048], P('prow', 'pcol'), may hold values from -0.0625 to 0.0625
- dinv: float32 [256, 2048], P(None, 'prow'), may hold values from -6 to 6
- rowblocks: int32 [8, 40], replicated, may hold values from 0 to 63, as said below
- counts: int32 [8], replicated, may hold values from 30 to 40
- widths: int32 [8], replicated, may hold values from 1 to 256, 1536 in all
Outputs:
- selected_inverse: bfloat16 [16384, 2048], P('pcol', 'prow')
- diagonal_blocks: float32 [256, 2048], P(None, 'prow')
Inputs may be any that keep to these rules, and one draw needn't show every extreme that they name: The entries of one row of rowblocks are distinct; only the first counts[k] entries of row k belong to supernode k. The widths sum to 1536.
All inputs are finite; a program needn't handle non-finite values.
Results may differ from a plain program's by a relative error of at most 0.02.
Values may be sent and summed in bfloat16 or wider, within the bound.
No kernel may reach another device: no remote copies, remote signals or barrier semaphores. Data moves between devices by JAX's collectives and lax.ppermute only.
A program may use at most 64 MiB of HBM per device.

v0:
```python
import jax
import jax.numpy as jnp
from jax import lax
from jax.sharding import PartitionSpec as P

B = 256
SNODES = 8


def from_root(value, axis, source):
    kept = jnp.where(lax.axis_index(axis) == source, value, 0).astype(value.dtype)
    return lax.psum(kept, axis)


def block_mask(block_ids, column_ids, rowblocks, counts, widths):
    slot_total = rowblocks.shape[1]
    owner_node = column_ids // B
    within = column_ids % B
    chosen = owner_node[:, None] == jnp.arange(SNODES, dtype=jnp.int32)[None, :]
    owner_rows = jnp.sum(jnp.where(chosen[:, :, None], rowblocks[None, :, :], 0), axis=1)
    owner_count = jnp.sum(jnp.where(chosen, counts[None, :], 0), axis=1)
    owner_width = jnp.sum(jnp.where(chosen, widths[None, :], 0), axis=1)
    slot_live = jnp.arange(slot_total, dtype=jnp.int32)[None, :] < owner_count[:, None]
    matched = (owner_rows[None, :, :] == block_ids[:, None, None]) & slot_live[None, :, :]
    present = jnp.any(matched, axis=2) & (within < owner_width)[None, :]
    return (present, owner_width, within)


def per_device(ainv, lpanel, dinv, rowblocks, counts, widths):
    row_group = lax.axis_index("prow")
    col_group = lax.axis_index("pcol")
    panel_rows = lpanel.shape[0]
    panel_cols = lpanel.shape[1]
    inverse_rows = ainv.shape[0]
    share_cols = dinv.shape[1]
    row_blocks = panel_rows // B
    col_blocks = inverse_rows // B
    own_ids = row_group * row_blocks + jnp.arange(row_blocks, dtype=jnp.int32)
    own_cols = col_group * panel_cols + jnp.arange(panel_cols, dtype=jnp.int32)
    present, unused_width, unused_within = block_mask(own_ids, own_cols, rowblocks, counts, widths)
    masked = jnp.where(
        present[:, None, :], lpanel.reshape(row_blocks, B, panel_cols), jnp.zeros((), jnp.bfloat16)
    )
    masked = masked.reshape(panel_rows, panel_cols)
    gathered = lax.all_gather(masked, "pcol", axis=1, tiled=True)
    product = jnp.dot(ainv, gathered, preferred_element_type=jnp.float32)
    root_row = col_group * col_blocks // row_blocks
    offset = (col_group * col_blocks - root_row * row_blocks) * B
    own_rows = lax.dynamic_slice_in_dim(gathered, offset, inverse_rows, 0)
    width_cols = max(share_cols, B)
    first_col = row_group * share_cols // width_cols * width_cols
    summed = lax.psum_scatter(
        product.astype(jnp.bfloat16), "prow", scatter_dimension=1, tiled=True
    ).astype(jnp.float32)
    whole_rows = from_root(own_rows, "prow", root_row)
    across = lax.dynamic_slice_in_dim(whole_rows, first_col, width_cols, 1)
    column_ids = row_group * share_cols + jnp.arange(share_cols, dtype=jnp.int32)
    block_ids = col_group * col_blocks + jnp.arange(col_blocks, dtype=jnp.int32)
    kept, owner_width, within = block_mask(block_ids, column_ids, rowblocks, counts, widths)
    negated = jnp.where(
        kept[:, None, :], -summed.reshape(col_blocks, B, share_cols), jnp.zeros((), jnp.float32)
    )
    selected_inverse = negated.reshape(inverse_rows, share_cols).astype(jnp.bfloat16)
    groups = max(1, share_cols // B)
    left_side = across.reshape(inverse_rows, groups, width_cols // groups).astype(jnp.float32)
    right_side = summed.reshape(inverse_rows, groups, share_cols // groups)
    quadratic = jnp.einsum(
        "rnb,rnc->bnc", left_side, right_side, precision=lax.Precision.HIGHEST
    ).reshape(B, share_cols)
    quadratic = lax.psum(quadratic.astype(jnp.bfloat16), "pcol").astype(jnp.float32)
    corner = (jnp.arange(B, dtype=jnp.int32)[:, None] < owner_width[None, :]) & (
        within < owner_width
    )[None, :]
    diagonal_blocks = jnp.where(corner, dinv, jnp.zeros((), jnp.float32)) + quadratic
    return (selected_inverse, diagonal_blocks)


def solution(mesh):
    placed = (P("pcol", "prow"), P("prow", "pcol"), P(None, "prow"), P(), P(), P())
    return jax.shard_map(
        per_device,
        mesh=mesh,
        in_specs=placed,
        out_specs=(P("pcol", "prow"), P(None, "prow")),
        check_vma=False,
    )
```

profile of v0, /device:TPU:24, one launch (start us, length us, event | category | flops | bytes accessed | tf_op | source)
XLA Modules:
  0.0 1071.4 jit_solution(718849329326859830)
XLA Ops:
  7.2 0.0 all-gather.2.cloned.1.call-start
  7.3 0.8 select_reduce_fusion.2
  8.1 0.8 select_reduce_fusion
  8.9 0.1 and_reduce_fusion
  9.1 0.1 copy.15
  9.2 0.1 broadcast_in_dim.155
  9.4 1.6 broadcast_select_fusion
  10.9 0.0 all-gather.2.cloned.1.call-update
  11.0 0.0 all-reduce.3.cloned.1.call-start
  11.0 240.8 %all-gather.2.cloned.1.call-done = bf16[1024,2048]{0,1:T(8,128)(2,1)} async-done(((bf16[1024,64]{0,1:T(8,128)(2,1)}), bf16[1024,2048]{0,1:T(8,128)(2,1)}) %all-gather.2.cloned.1.call-update) | async-done | bytes 4194320 | tf_op jit(solution)/shard_map/all_gather | solution.py:45
  251.9 3.3 dynamic-slice_select_fusion
  255.2 0.0 all-reduce.3.cloned.1.call-update
  255.2 0.0 reduce-scatter.2.cloned.1.call-start
  255.3 6.0 fusion
  261.2 0.0 reduce-scatter.2.cloned.1.call-update
  261.3 0.0 all-reduce.5.cloned.1.call-start
  261.4 0.5 copy-done.3
  261.9 0.0 copy-done.4
  261.9 0.1 select_reduce_fusion.4
  262.0 0.1 select_reduce_fusion.1
  262.1 0.1 and_reduce_fusion.1
  262.3 0.2 copy.16
  262.5 0.1 copy.17
  262.6 262.5 %all-reduce.3.cloned.1.call-done = bf16[512,2048]{0,1:T(8,128)(2,1)} async-done(((bf16[512,2048]{0,1:T(8,128)(2,1)}), bf16[512,2048]{0,1:T(8,128)(2,1)}) %all-reduce.3.cloned.1.call-update) | async-done | bytes 2097168 | tf_op jit(solution)/shard_map/psum | solution.py:12
  525.0 130.8 %reduce-scatter.2.cloned.1.call-done = bf16[512,128]{0,1:T(8,128)(2,1)} async-done(((bf16[512,2048]{0,1:T(8,128)(2,1)}), bf16[512,128]{0,1:T(8,128)(2,1)}) %reduce-scatter.2.cloned.1.call-update) | async-done | bytes 131088 | tf_op jit(solution)/shard_map/reduce_scatter | solution.py:52
  655.8 1.9 fusion.1
  657.7 0.0 all-reduce.5.cloned.1.call-update
  657.7 1.0 select_convert_fusion
  658.7 0.8 copy.18
  659.4 403.7 %all-reduce.5.cloned.1.call-done = bf16[256,128]{0,1:T(8,128)(2,1)} async-done(((bf16[256,128]{0,1:T(8,128)(2,1)}), bf16[256,128]{0,1:T(8,128)(2,1)}) %all-reduce.5.cloned.1.call-update) | async-done | bytes 65552 | tf_op jit(solution)/shard_map/psum | solution.py:70
  1063.1 0.9 convert_add_fusion
  1064.1 0.8 copy.19
  (22 shorter events, 0.2 us)
Async XLA Ops:
  7.2 248.1 %copy-start = (bf16[512,1024]{1,0:T(8,128)(2,1)S(1)}, bf16[512,1024]{1,0:T(8,128)(2,1)}, u32[]{:S(2)}) copy-start(bf16[512,1024]{1,0:T(8,128)(2,1)} %param.6) | copy-start | bytes 3145732
  7.2 244.7 %all-gather.2.cloned.1.call-start = ((), (), s32[]{:S(2)}) async-start(), calls=%async_computation.1 | async-start | bytes 4325376 | tf_op jit(solution)/shard_map/all_gather | solution.py:45
  11.0 514.1 %all-reduce.3.cloned.1.call-start = ((), (), s32[]{:S(2)}) async-start(), calls=%async_computation.3 | async-start | bytes 4194304 | tf_op jit(solution)/shard_map/psum | solution.py:12
  255.2 400.6 %reduce-scatter.2.cloned.1.call-start = ((), (), s32[]{:S(2)}) async-start(), calls=%async_computation.2 | async-start | bytes 2228224 | tf_op jit(solution)/shard_map/reduce_scatter | solution.py:52
  261.2 0.7 copy-start.3
  261.2 0.7 copy-start.4
  261.2 0.8 copy-start.2
  261.2 1.2 copy-start.1
  261.3 801.9 %all-reduce.5.cloned.1.call-start = ((), (), s32[]{:S(2)}) async-start(), calls=%async_computation.4 | async-start | bytes 131072 | tf_op jit(solution)/shard_map/psum | solution.py:70
Sparse Core Ops, SparseCore 0:
  11.1 240.7 all-gather.1
  255.3 269.6 all-reduce.2
  529.9 125.8 reduce-scatter.1
  659.1 403.9 all-reduce.4
where the time goes:
time: 1070 us
  waiting for transfers between devices  1040 us (97%)
  between operations  14 us (1%)
    psum x1, waiting for transfers between devices, per_device(): lax.psum(quadratic.astype(jnp.bfloat16), 'pcol').astype(jnp.float32)  404 us
    psum x1, waiting for transfers between devices, from_root(): return lax.psum(kept, axis)  262 us
    all_gather x1, waiting for transfers between devices, per_device(): gathered = lax.all_gather(masked, 'pcol', axis=1, tiled=True)  241 us
    reduce_scatter x1, waiting for transfers between devices, per_device(): lax.psum_scatter(product.astype(jnp.bfloat16), 'prow', scatter_dimension=...  131 us
  transfers between devices with their start and end apart: 4, of which 4 were waited for; matrix products, arithmetic and copies ran while one was open for 1% of the time, Pallas kernels for 0%

commit v1 on v0

v1 whole, which is shorter than its diff:
```python
import jax
import jax.numpy as jnp
from jax import lax
from jax.sharding import PartitionSpec as P

B = 256
SNODES = 8
AXES = ("prow", "pcol")
CONTRACT_LAST = (((1,), (1,)), ((), ()))


def send(value, target):
    pairs = []
    for source in range(512):
        row, col = source // 32, source % 32
        zh, y, core, x, zl = target(row >> 3, (row >> 1) & 3, row & 1, col >> 3, col & 7)
        pairs.append((source, ((zh * 4 + y) * 2 + core) * 32 + x * 8 + zl))
    return lax.ppermute(value, AXES, pairs)


def fold_x(zh, y, core, x, zl, flip):
    node = 2 * x + (zl >> 2)
    return (zh, y, core, node & 3, (((node >> 2) ^ flip) << 2) | (zl & 3))


def rows_home(zh, y, core, x, zl):
    return (zl >> 2, x, (zl >> 1) & 1, (zh << 1) | (y >> 1), ((y & 1) << 2) | (core << 1) | (zl & 1))


def dot_t(left, right):
    return lax.dot_general(left, right, CONTRACT_LAST, preferred_element_type=jnp.float32)


def flip_if(value, bit, axis):
    return jnp.where(bit == 0, value, jnp.flip(value, axis))


def per_device(ainv, lpanel, dinv, rowblocks, counts, widths):
    prow, pcol = lax.axis_index("prow"), lax.axis_index("pcol")
    zh, y, core = prow >> 3, (prow >> 1) & 3, prow & 1
    x, zl = pcol >> 3, pcol & 7
    high, mid, low = zl >> 2, (zl >> 1) & 1, zl & 1

    own = lpanel.T
    first = send(own, lambda *d: fold_x(*d, 0))
    second = send(own, lambda *d: fold_x(*d, 1))
    pair = jnp.stack([first, second])
    near = send(pair, lambda zh, y, core, x, zl: (zh, y, core, x, zl ^ 2))
    quad = jnp.stack([pair, near], axis=1)
    last = send(quad, lambda zh, y, core, x, zl: (zh, y, core, x, zl ^ 1))

    a1 = send(ainv, lambda zh, y, core, x, zl: (zh, y, core, x ^ 1, zl))
    a3 = send(ainv, lambda zh, y, core, x, zl: (zh, y, core, x ^ 3, zl))
    half = ainv.shape[0] // 2
    a2 = [
        send(a3[:half], lambda zh, y, core, x, zl: (zh, y, core, x ^ 1, zl)),
        send(a1[half:], lambda zh, y, core, x, zl: (zh, y, core, x ^ 3, zl)),
    ]
    a2 = jnp.concatenate(a2, axis=0)

    slots = jnp.arange(rowblocks.shape[1], dtype=jnp.int32)
    used = jnp.where(slots[None, :] < counts[:, None], rowblocks, -1)
    member = jnp.any(used[:, :, None] == jnp.arange(64, dtype=jnp.int32)[None, None, :], axis=1)
    nodes = jnp.arange(SNODES, dtype=jnp.int32)
    my_nodes = (high ^ jnp.arange(2, dtype=jnp.int32)) * 4 + x
    chosen = my_nodes[:, None] == nodes[None, :]
    my_blocks = prow * 4 + jnp.arange(4, dtype=jnp.int32)
    block_is = my_blocks[:, None] == jnp.arange(64, dtype=jnp.int32)[None, :]
    live = jnp.any(
        chosen[:, None, :, None] & block_is[None, :, None, :] & member[None, None, :, :], axis=(2, 3)
    )
    width = jnp.sum(jnp.where(chosen, widths[None, :], 0), axis=1)
    quarter = (
        (mid ^ jnp.arange(2, dtype=jnp.int32))[:, None] * 2
        + (low ^ jnp.arange(2, dtype=jnp.int32))[None, :]
    )
    within = quarter[:, :, None] * 64 + jnp.arange(64, dtype=jnp.int32)[None, None, :]
    active = within[None] < width[:, None, None, None]

    factor = jnp.stack([quad, last], axis=2)
    keep_mask = active[..., None, None] & live[:, None, None, None, :, None]
    factor = jnp.where(
        keep_mask, factor.reshape(2, 2, 2, 64, 4, B), jnp.zeros((), jnp.bfloat16)
    ).reshape(2, 2, 2, 64, 1024)

    mine = lax.dynamic_slice_in_dim(factor[0], low * 512, 512, axis=3)
    across = send(mine, rows_home)

    keep = core ^ mid
    theirs = lax.dynamic_index_in_dim(factor, 1 - keep, 1, keepdims=False).reshape(256, 1024)
    ours = lax.dynamic_index_in_dim(factor, keep, 1, keepdims=False).reshape(256, 1024)
    blocks = [ainv, a1, a2, a3]
    away = jnp.stack([dot_t(theirs, block).astype(jnp.bfloat16) for block in blocks])
    other = send(away, lambda zh, y, core, x, zl: (zh, y, core ^ 1, x, zl))
    here = jnp.stack([dot_t(ours, block) for block in blocks])
    chip = (here + other.astype(jnp.float32)).astype(jnp.bfloat16)

    total = None
    for k in range(4):
        share = lax.dynamic_index_in_dim(chip, y ^ k ^ x, 0, keepdims=False)
        came = send(share, lambda zh, y, core, x, zl: (zh, x, core, y ^ k, zl)).astype(jnp.float32)
        total = came if total is None else total + came
    total = total.reshape(2, 128, 512)

    stay = zh ^ high
    leave = lax.dynamic_index_in_dim(total, 1 - stay, 0, keepdims=False).astype(jnp.bfloat16)
    came = send(leave, lambda zh, y, core, x, zl: (zh ^ 1, y, core, x, zl))
    product = lax.dynamic_index_in_dim(total, stay, 0, keepdims=False) + came.astype(jnp.float32)
    product = flip_if(product.reshape(2, 64, 512), low, 0).reshape(128, 512)

    node = prow >> 1
    row_ids = pcol * 2 + jnp.arange(2, dtype=jnp.int32)
    kept = jnp.any(
        (row_ids[:, None] == jnp.arange(64, dtype=jnp.int32)[None, :])[:, None, :]
        & (nodes == node)[None, :, None]
        & member[None],
        axis=(1, 2),
    )
    negated = jnp.where(kept[None, :, None], -product.reshape(128, 2, B), 0.0).reshape(128, 512)
    selected_inverse = negated.astype(jnp.bfloat16).T

    terms = dot_t(across.reshape(256, 512), product.astype(jnp.bfloat16))
    terms = flip_if(flip_if(terms.reshape(2, 2, 64, 128), low, 1), core, 0).reshape(256, 128)
    terms = terms.astype(jnp.bfloat16)
    by_x = [terms] + [
        send(terms, lambda zh, y, core, x, zl: (zh, y, core, x ^ k, zl)) for k in (1, 2, 3)
    ]
    by_x = [part.astype(jnp.float32) for part in by_x]
    terms = (by_x[0] + by_x[1]) + (by_x[2] + by_x[3])
    for bit in (4, 2, 1):
        sent = terms.astype(jnp.bfloat16)
        came = send(sent, lambda zh, y, core, x, zl: (zh, y, core, x, zl ^ bit))
        terms = sent.astype(jnp.float32) + came.astype(jnp.float32)

    my_width = jnp.sum(jnp.where(nodes == node, widths, 0))
    column = core * 128 + jnp.arange(128, dtype=jnp.int32)
    corner = (jnp.arange(B, dtype=jnp.int32)[:, None] < my_width) & (column < my_width)[None, :]
    diagonal_blocks = jnp.where(corner, dinv, 0.0) + terms
    return (selected_inverse, diagonal_blocks)


def solution(mesh):
    placed = (P("pcol", "prow"), P("prow", "pcol"), P(None, "prow"), P(), P(), P())
    return jax.shard_map(
        per_device,
        mesh=mesh,
        in_specs=placed,
        out_specs=(P("pcol", "prow"), P(None, "prow")),
        check_vma=False,
    )
```

time: 1070 us -> 206 us (0.19)
  waiting for transfers between devices: 1040 us -> 78.6 us
  starting transfers between devices: 0.16 us -> 98 us
  between operations: 14 us -> 1.28 us
    psum x2 -> x0, waiting for transfers between devices: 666 us -> none  [the longest x1 404 us: per_device(): lax.psum(quadratic.astype(jnp.bfloat16), 'pcol').astype(jnp.float32)]
    all_gather x1 -> x0, waiting for transfers between devices: 241 us -> none  [per_device(): gathered = lax.all_gather(masked, 'pcol', axis=1, tiled=True)]
    reduce_scatter x1 -> x0, waiting for transfers between devices: 131 us -> none  [per_device(): lax.psum_scatter(product.astype(jnp.bfloat16), 'prow', scatter_dimension=...]
    ppermute x0 -> x21, starting transfers between devices: none -> 98 us  [send(): return lax.ppermute(value, AXES, pairs)]
    ppermute x0 -> x21, waiting for transfers between devices: none -> 78.6 us  [send(): return lax.ppermute(value, AXES, pairs)]
  transfers between devices with their start and end apart: 4 -> 21, of which waited for: 4 -> 12; matrix products, arithmetic and copies ran while one was open for 1% -> 9% of each run, Pallas kernels for 0% -> 0%
where the time goes in v1:
time: 206 us; the launch traced here: 204 us
  starting transfers between devices  98 us (48%)
  waiting for transfers between devices  78.6 us (38%)
  other arithmetic  11.6 us (6%)
  local copies, waits for them, and re-layouts  9.05 us (4%)
  matrix products  5.25 us (3%)
    ppermute x21, starting transfers between devices, send(): return lax.ppermute(value, AXES, pairs)  98 us
    ppermute x21, waiting for transfers between devices, send(): return lax.ppermute(value, AXES, pairs)  78.6 us
    dot_general x9, matrix products, dot_t(): lax.dot_general(left, right, CONTRACT_LAST, preferred_element_type=jnp.fl...  5.25 us
    broadcast_in_dim x2, local copies, waits for them, and re-layouts, per_device(): jnp.where(keep_mask, factor.reshape(2, 2, 2, 64, 4, B), jnp.zeros((), jnp...  4.33 us
  transfers between devices with their start and end apart: 21, of which 12 were waited for; matrix products, arithmetic and copies ran while one was open for 9% of the time, Pallas kernels for 0%

profile of v1, /device:TPU:24, one launch (start us, length us, event | category | flops | bytes accessed | tf_op | source)
XLA Modules:
  0.0 203.8 jit_solution(10161616657550559850)
XLA Ops:
  0.6 9.1 %collective-permute-start.1 = (bf16[64,1024]{1,0:T(8,128)(2,1)}, bf16[64,1024]{1,0:T(8,128)(2,1)S(1)}, u32[]{:S(2)}, u32[]{:S(2)}) collective-permute-start(bf16[64,1024]{1,0:T(8,128)(2,1)} %bitcast.99), channel_id=1, source_target_pairs={{0,4},{1,5},{2,6},{3,7},{4,12},{5,13},{6,14},{7,15},{8,20},{9,21},... | collective-permute-start | bytes 393224 | tf_op jit(solution)/shard_map/ppermute | solution.py:18
  11.3 4.7 %collective-permute-start.4 = (bf16[512,1024]{1,0:T(8,128)(2,1)}, bf16[512,1024]{1,0:T(8,128)(2,1)S(1)}, u32[]{:S(2)}, u32[]{:S(2)}) collective-permute-start(bf16[512,1024]{1,0:T(8,128)(2,1)} %param.6), channel_id=1, source_target_pairs={{0,8},{1,9},{2,10},{3,11},{4,12},{5,13},{6,14},{7,15},{8,0},{9,1},... | collective-permute-start | bytes 3145736 | tf_op jit(solution)/shard_map/ppermute | solution.py:18
  16.0 4.5 %collective-permute-start.5 = (bf16[512,1024]{1,0:T(8,128)(2,1)}, bf16[512,1024]{1,0:T(8,128)(2,1)S(1)}, u32[]{:S(2)}, u32[]{:S(2)}) collective-permute-start(bf16[512,1024]{1,0:T(8,128)(2,1)} %param.6), channel_id=1, source_target_pairs={{0,24},{1,25},{2,26},{3,27},{4,28},{5,29},{6,30},{7,31},{8,16},{9,... | collective-permute-start | bytes 3145736 | tf_op jit(solution)/shard_map/ppermute | solution.py:18
  21.7 5.2 %collective-permute-start.2 = (bf16[2,64,1024]{2,1,0:T(8,128)(2,1)S(1)}, bf16[2,64,1024]{2,1,0:T(8,128)(2,1)S(1)}, u32[]{:S(2)}, u32[]{:S(2)}) collective-permute-start(bf16[2,64,1024]{2,1,0:T(8,128)(2,1)S(1)} %get-tuple-element.17), channel_id=1, source_target_pairs={{0,2},{1,3},{2,0},{3,1},{4,6},{5,7},{6,4},{7,5},{8,10},{9,11},{10,... | collective-permute-start | bytes 786440 | tf_op jit(solution)/shard_map/ppermute | solution.py:18
  27.3 13.1 %collective-permute-done.2 = bf16[2,64,1024]{2,1,0:T(8,128)(2,1)S(1)} collective-permute-done((bf16[2,64,1024]{2,1,0:T(8,128)(2,1)S(1)}, bf16[2,64,1024]{2,1,0:T(8,128)(2,1)S(1)}, u32[]{:S(2)}, u32[]{:S(2)}) %collective-permute-start.2) | collective-permute-done | bytes 262176 | tf_op jit(solution)/shard_map/ppermute | solution.py:18
  46.2 2.4 %reshape.197 = pred[2,2,2,64,1024]{4,3,2,1,0:T(8,128)(4,1)} reshape(pred[2,2,2,64,4,256]{5,4,3,2,1,0:T(4,128)(4,1)} %broadcast_in_dim.90) | data formatting | bytes 1048576 | tf_op jit(solution)/shard_map/jit(_where)/broadcast_in_dim | solution.py:82
  48.6 6.9 %collective-permute-done.3 = bf16[2,2,64,1024]{3,2,0,1:T(8,128)(2,1)S(1)} collective-permute-done((bf16[2,2,64,1024]{3,2,0,1:T(8,128)(2,1)}, bf16[2,2,64,1024]{3,2,0,1:T(8,128)(2,1)S(1)}, u32[]{:S(2)}, u32[]{:S(2)}) %collective-permute-start.3) | collective-permute-done | bytes 524320 | tf_op jit(solution)/shard_map/ppermute | solution.py:18
  56.9 6.8 %collective-permute-start.7 = (bf16[256,1024]{1,0:T(8,128)(2,1)S(1)}, bf16[256,1024]{1,0:T(8,128)(2,1)S(1)}, u32[]{:S(2)}, u32[]{:S(2)}) collective-permute-start(bf16[256,1024]{1,0:T(8,128)(2,1)S(1)} %slice.14), channel_id=1, source_target_pairs={{0,24},{1,25},{2,26},{3,27},{4,28},{5,29},{6,30},{7,31},{8,16},{9,... | collective-permute-start | bytes 1572872 | tf_op jit(solution)/shard_map/ppermute | solution.py:18
  63.8 1.9 collective-permute-start.6
  67.2 11.2 %collective-permute-done.6 = bf16[256,1024]{1,0:T(8,128)(2,1)S(1)} collective-permute-done((bf16[256,1024]{1,0:T(8,128)(2,1)S(1)}, bf16[256,1024]{1,0:T(8,128)(2,1)S(1)}, u32[]{:S(2)}, u32[]{:S(2)}) %collective-permute-start.6) | collective-permute-done | bytes 524320 | tf_op jit(solution)/shard_map/ppermute | solution.py:18
  81.1 1.9 collective-permute-start.8
  88.6 1.9 collective-permute-start.9
  90.5 1.9 collective-permute-start.12
  92.5 8.1 %collective-permute-start.11 = (bf16[256,512]{1,0:T(8,128)(2,1)S(1)}, bf16[256,512]{1,0:T(8,128)(2,1)}, u32[]{:S(2)}, u32[]{:S(2)}) collective-permute-start(bf16[256,512]{1,0:T(8,128)(2,1)S(1)} %get-tuple-element.8), channel_id=1, source_target_pairs={{0,16},{1,17},{2,18},{3,19},{4,20},{5,21},{6,22},{7,23},{8,80},{9,... | collective-permute-start | bytes 786440 | tf_op jit(solution)/shard_map/ppermute | solution.py:18
  100.6 1.9 collective-permute-start.10
  103.7 4.5 %collective-permute-done.9 = bf16[256,512]{1,0:T(8,128)(2,1)S(1)} collective-permute-done((bf16[256,512]{1,0:T(8,128)(2,1)S(1)}, bf16[256,512]{1,0:T(8,128)(2,1)S(1)}, u32[]{:S(2)}, u32[]{:S(2)}) %collective-permute-start.9) | collective-permute-done | bytes 262176 | tf_op jit(solution)/shard_map/ppermute | solution.py:18
  108.2 3.8 %collective-permute-done.11 = bf16[256,512]{1,0:T(8,128)(2,1)} collective-permute-done((bf16[256,512]{1,0:T(8,128)(2,1)S(1)}, bf16[256,512]{1,0:T(8,128)(2,1)}, u32[]{:S(2)}, u32[]{:S(2)}) %collective-permute-start.11) | collective-permute-done | bytes 262176 | tf_op jit(solution)/shard_map/ppermute | solution.py:18
  112.0 7.7 %collective-permute-done.10 = bf16[256,512]{1,0:T(8,128)(2,1)} collective-permute-done((bf16[256,512]{1,0:T(8,128)(2,1)S(1)}, bf16[256,512]{1,0:T(8,128)(2,1)}, u32[]{:S(2)}, u32[]{:S(2)}) %collective-permute-start.10) | collective-permute-done | bytes 262176 | tf_op jit(solution)/shard_map/ppermute | solution.py:18
  121.0 14.0 %collective-permute-start.13 = (bf16[128,512]{1,0:T(8,128)(2,1)S(1)}, bf16[128,512]{1,0:T(8,128)(2,1)S(1)}, u32[]{:S(2)}, u32[]{:S(2)}) collective-permute-start(bf16[128,512]{1,0:T(8,128)(2,1)S(1)} %fusion.11), channel_id=1, source_target_pairs={{0,256},{1,257},{2,258},{3,259},{4,260},{5,261},{6,262},{7,263},{8... | collective-permute-start | bytes 393224 | tf_op jit(solution)/shard_map/ppermute | solution.py:18
  136.0 1.9 collective-permute-start.14
  137.9 3.4 %collective-permute-done.13 = bf16[128,512]{1,0:T(8,128)(2,1)S(1)} collective-permute-done((bf16[128,512]{1,0:T(8,128)(2,1)S(1)}, bf16[128,512]{1,0:T(8,128)(2,1)S(1)}, u32[]{:S(2)}, u32[]{:S(2)}) %collective-permute-start.13) | collective-permute-done | bytes 131104 | tf_op jit(solution)/shard_map/ppermute | solution.py:18
  141.4 11.6 %collective-permute-done.14 = bf16[2,2,64,512]{3,2,1,0:T(8,128)(2,1)S(1)} collective-permute-done((bf16[2,2,64,512]{3,2,1,0:T(8,128)(2,1)S(1)}, bf16[2,2,64,512]{3,2,1,0:T(8,128)(2,1)S(1)}, u32[]{:S(2)}, u32[]{:S(2)}) %collective-permute-start.14) | collective-permute-done | bytes 262176 | tf_op jit(solution)/shard_map/ppermute | solution.py:18
  153.3 4.1 %collective-permute-start.16 = (bf16[256,128]{1,0:T(8,128)(2,1)S(1)}, bf16[256,128]{1,0:T(8,128)(2,1)S(1)}, u32[]{:S(2)}, u32[]{:S(2)}) collective-permute-start(bf16[256,128]{1,0:T(8,128)(2,1)S(1)} %bitcast.96), channel_id=1, source_target_pairs={{0,16},{1,17},{2,18},{3,19},{4,20},{5,21},{6,22},{7,23},{8,24},{9,... | collective-permute-start | bytes 196616 | tf_op jit(solution)/shard_map/ppermute | solution.py:18
  157.4 6.6 %collective-permute-start.15 = (bf16[256,128]{1,0:T(8,128)(2,1)S(1)}, bf16[256,128]{1,0:T(8,128)(2,1)S(1)}, u32[]{:S(2)}, u32[]{:S(2)}) collective-permute-start(bf16[256,128]{1,0:T(8,128)(2,1)S(1)} %bitcast.97), channel_id=1, source_target_pairs={{0,8},{1,9},{2,10},{3,11},{4,12},{5,13},{6,14},{7,15},{8,0},{9,1},... | collective-permute-start | bytes 196616 | tf_op jit(solution)/shard_map/ppermute | solution.py:18
  164.0 1.9 collective-permute-start.17
  166.6 4.8 %collective-permute-done.17 = bf16[256,128]{1,0:T(8,128)(2,1)S(1)} collective-permute-done((bf16[256,128]{1,0:T(8,128)(2,1)S(1)}, bf16[256,128]{1,0:T(8,128)(2,1)S(1)}, u32[]{:S(2)}, u32[]{:S(2)}) %collective-permute-start.17) | collective-permute-done | bytes 65568 | tf_op jit(solution)/shard_map/ppermute | solution.py:18
  171.4 14.0 %collective-permute-start.18 = (bf16[256,128]{1,0:T(8,128)(2,1)S(1)}, bf16[256,128]{1,0:T(8,128)(2,1)S(1)}, u32[]{:S(2)}, u32[]{:S(2)}) collective-permute-start(bf16[256,128]{1,0:T(8,128)(2,1)S(1)} %add_convert_fusion.2), channel_id=1, source_target_pairs={{0,4},{1,5},{2,6},{3,7},{4,0},{5,1},{6,2},{7,3},{8,12},{9,13},{10,... | collective-permute-start | bytes 196616 | tf_op jit(solution)/shard_map/ppermute | solution.py:18
  186.1 3.7 %collective-permute-done.18 = bf16[256,128]{1,0:T(8,128)(2,1)S(1)} collective-permute-done((bf16[256,128]{1,0:T(8,128)(2,1)S(1)}, bf16[256,128]{1,0:T(8,128)(2,1)S(1)}, u32[]{:S(2)}, u32[]{:S(2)}) %collective-permute-start.18) | collective-permute-done | bytes 65568 | tf_op jit(solution)/shard_map/ppermute | solution.py:18
  189.8 2.0 collective-permute-start.19
  192.5 4.4 %collective-permute-done.19 = bf16[256,128]{1,0:T(8,128)(2,1)S(1)} collective-permute-done((bf16[256,128]{1,0:T(8,128)(2,1)S(1)}, bf16[256,128]{1,0:T(8,128)(2,1)S(1)}, u32[]{:S(2)}, u32[]{:S(2)}) %collective-permute-start.19) | collective-permute-done | bytes 65568 | tf_op jit(solution)/shard_map/ppermute | solution.py:18
  196.9 1.9 collective-permute-start.20
  199.6 3.4 %collective-permute-done.20 = bf16[256,128]{1,0:T(8,128)(2,1)S(1)} collective-permute-done((bf16[256,128]{1,0:T(8,128)(2,1)S(1)}, bf16[256,128]{1,0:T(8,128)(2,1)S(1)}, u32[]{:S(2)}, u32[]{:S(2)}) %collective-permute-start.20) | collective-permute-done | bytes 65568 | tf_op jit(solution)/shard_map/ppermute | solution.py:18
  (91 shorter events, 27.0 us)
Async XLA Ops:
  0.6 21.0 %collective-permute-start.1 = (bf16[64,1024]{1,0:T(8,128)(2,1)}, bf16[64,1024]{1,0:T(8,128)(2,1)S(1)}, u32[]{:S(2)}, u32[]{:S(2)}) collective-permute-start(bf16[64,1024]{1,0:T(8,128)(2,1)} %bitcast.99), channel_id=1, source_target_pairs={{0,4},{1,5},{2,6},{3,7},{4,12},{5,13},{6,14},{7,15},{8,20},{9,21},... | collective-permute-start | bytes 393224 | tf_op jit(solution)/shard_map/ppermute | solution.py:18
  9.7 11.9 %collective-permute-start = (bf16[64,1024]{1,0:T(8,128)(2,1)}, bf16[64,1024]{1,0:T(8,128)(2,1)S(1)}, u32[]{:S(2)}, u32[]{:S(2)}) collective-permute-start(bf16[64,1024]{1,0:T(8,128)(2,1)} %bitcast.100), channel_id=1, source_target_pairs={{0,0},{1,1},{2,2},{3,3},{4,8},{5,9},{6,10},{7,11},{8,16},{9,17},{1... | collective-permute-start | bytes 393224 | tf_op jit(solution)/shard_map/ppermute | solution.py:18
  11.3 45.5 %collective-permute-start.4 = (bf16[512,1024]{1,0:T(8,128)(2,1)}, bf16[512,1024]{1,0:T(8,128)(2,1)S(1)}, u32[]{:S(2)}, u32[]{:S(2)}) collective-permute-start(bf16[512,1024]{1,0:T(8,128)(2,1)} %param.6), channel_id=1, source_target_pairs={{0,8},{1,9},{2,10},{3,11},{4,12},{5,13},{6,14},{7,15},{8,0},{9,1},... | collective-permute-start | bytes 3145736 | tf_op jit(solution)/shard_map/ppermute | solution.py:18
  16.0 47.7 %collective-permute-start.5 = (bf16[512,1024]{1,0:T(8,128)(2,1)}, bf16[512,1024]{1,0:T(8,128)(2,1)S(1)}, u32[]{:S(2)}, u32[]{:S(2)}) collective-permute-start(bf16[512,1024]{1,0:T(8,128)(2,1)} %param.6), channel_id=1, source_target_pairs={{0,24},{1,25},{2,26},{3,27},{4,28},{5,29},{6,30},{7,31},{8,16},{9,... | collective-permute-start | bytes 3145736 | tf_op jit(solution)/shard_map/ppermute | solution.py:18
  21.7 19.7 %copy-start.3 = (bf16[64,1024]{1,0:T(8,128)(2,1)}, bf16[64,1024]{1,0:T(8,128)(2,1)S(1)}, u32[]{:S(2)}) copy-start(bf16[64,1024]{1,0:T(8,128)(2,1)S(1)} %collective-permute-done) | copy-start | bytes 393220
  21.7 21.6 %copy-start.7 = (s32[8]{0:T(128)S(1)}, s32[8]{0:T(128)}, u32[]{:S(2)}) copy-start(s32[8]{0:T(128)} %param.11) | copy-start | bytes 100
  21.7 18.7 %collective-permute-start.2 = (bf16[2,64,1024]{2,1,0:T(8,128)(2,1)S(1)}, bf16[2,64,1024]{2,1,0:T(8,128)(2,1)S(1)}, u32[]{:S(2)}, u32[]{:S(2)}) collective-permute-start(bf16[2,64,1024]{2,1,0:T(8,128)(2,1)S(1)} %get-tuple-element.17), channel_id=1, source_target_pairs={{0,2},{1,3},{2,0},{3,1},{4,6},{5,7},{6,4},{7,5},{8,10},{9,11},{10,... | collective-permute-start | bytes 786440 | tf_op jit(solution)/shard_map/ppermute | solution.py:18
  41.3 14.2 %collective-permute-start.3 = (bf16[2,2,64,1024]{3,2,0,1:T(8,128)(2,1)}, bf16[2,2,64,1024]{3,2,0,1:T(8,128)(2,1)S(1)}, u32[]{:S(2)}, u32[]{:S(2)}) collective-permute-start(bf16[2,2,64,1024]{3,2,0,1:T(8,128)(2,1)} %get-tuple-element.13), channel_id=1, source_target_pairs={{0,1},{1,0},{2,3},{3,2},{4,5},{5,4},{6,7},{7,6},{8,9},{9,8},{10,11... | collective-permute-start | bytes 1572872 | tf_op jit(solution)/shard_map/ppermute | solution.py:18
  43.7 0.6 copy-start.5
  56.8 8.9 %copy-start.2 = (bf16[512,1024]{1,0:T(8,128)(2,1)S(1)}, bf16[512,1024]{1,0:T(8,128)(2,1)}, u32[]{:S(2)}) copy-start(bf16[512,1024]{1,0:T(8,128)(2,1)} %param.6) | copy-start | bytes 3145732
  56.9 21.5 %collective-permute-start.7 = (bf16[256,1024]{1,0:T(8,128)(2,1)S(1)}, bf16[256,1024]{1,0:T(8,128)(2,1)S(1)}, u32[]{:S(2)}, u32[]{:S(2)}) collective-permute-start(bf16[256,1024]{1,0:T(8,128)(2,1)S(1)} %slice.14), channel_id=1, source_target_pairs={{0,24},{1,25},{2,26},{3,27},{4,28},{5,29},{6,30},{7,31},{8,16},{9,... | collective-permute-start | bytes 1572872 | tf_op jit(solution)/shard_map/ppermute | solution.py:18
  63.8 14.6 %collective-permute-start.6 = (bf16[256,1024]{1,0:T(8,128)(2,1)S(1)}, bf16[256,1024]{1,0:T(8,128)(2,1)S(1)}, u32[]{:S(2)}, u32[]{:S(2)}) collective-permute-start(bf16[256,1024]{1,0:T(8,128)(2,1)S(1)} %slice.13), channel_id=1, source_target_pairs={{0,8},{1,9},{2,10},{3,11},{4,12},{5,13},{6,14},{7,15},{8,0},{9,1},... | collective-permute-start | bytes 1572872 | tf_op jit(solution)/shard_map/ppermute | solution.py:18
  78.5 1.0 copy-start
  81.1 5.9 %collective-permute-start.8 = (bf16[4,256,512]{2,1,0:T(8,128)(2,1)}, bf16[4,256,512]{2,1,0:T(8,128)(2,1)}, u32[]{:S(2)}, u32[]{:S(2)}) collective-permute-start(bf16[4,256,512]{2,1,0:T(8,128)(2,1)} %pad_maximum_fusion), channel_id=1, source_target_pairs={{0,32},{1,33},{2,34},{3,35},{4,36},{5,37},{6,38},{7,39},{8,40},{9,... | collective-permute-start | bytes 3145736 | tf_op jit(solution)/shard_map/ppermute | solution.py:18
  85.2 1.2 copy-start.1
  88.5 14.5 %copy-start.4 = (bf16[64,1024]{1,0:T(8,128)(2,1)S(1)}, bf16[64,1024]{1,0:T(8,128)(2,1)}, u32[]{:S(2)}) copy-start(bf16[64,1024]{1,0:T(8,128)(2,1)} %copy-done.3) | copy-start | bytes 393220
  88.6 19.6 %collective-permute-start.9 = (bf16[256,512]{1,0:T(8,128)(2,1)S(1)}, bf16[256,512]{1,0:T(8,128)(2,1)S(1)}, u32[]{:S(2)}, u32[]{:S(2)}) collective-permute-start(bf16[256,512]{1,0:T(8,128)(2,1)S(1)} %get-tuple-element.6), channel_id=1, source_target_pairs={{0,0},{1,1},{2,2},{3,3},{4,4},{5,5},{6,6},{7,7},{8,64},{9,65},{10,... | collective-permute-start | bytes 786440 | tf_op jit(solution)/shard_map/ppermute | solution.py:18
  90.5 17.6 %collective-permute-start.12 = (bf16[256,512]{1,0:T(8,128)(2,1)S(1)}, bf16[256,512]{1,0:T(8,128)(2,1)}, u32[]{:S(2)}, u32[]{:S(2)}) collective-permute-start(bf16[256,512]{1,0:T(8,128)(2,1)S(1)} %get-tuple-element.7), channel_id=1, source_target_pairs={{0,24},{1,25},{2,26},{3,27},{4,28},{5,29},{6,30},{7,31},{8,88},{9,... | collective-permute-start | bytes 786440 | tf_op jit(solution)/shard_map/ppermute | solution.py:18
  92.5 19.5 %collective-permute-start.11 = (bf16[256,512]{1,0:T(8,128)(2,1)S(1)}, bf16[256,512]{1,0:T(8,128)(2,1)}, u32[]{:S(2)}, u32[]{:S(2)}) collective-permute-start(bf16[256,512]{1,0:T(8,128)(2,1)S(1)} %get-tuple-element.8), channel_id=1, source_target_pairs={{0,16},{1,17},{2,18},{3,19},{4,20},{5,21},{6,22},{7,23},{8,80},{9,... | collective-permute-start | bytes 786440 | tf_op jit(solution)/shard_map/ppermute | solution.py:18
  100.6 19.1 %collective-permute-start.10 = (bf16[256,512]{1,0:T(8,128)(2,1)S(1)}, bf16[256,512]{1,0:T(8,128)(2,1)}, u32[]{:S(2)}, u32[]{:S(2)}) collective-permute-start(bf16[256,512]{1,0:T(8,128)(2,1)S(1)} %get-tuple-element.9), channel_id=1, source_target_pairs={{0,8},{1,9},{2,10},{3,11},{4,12},{5,13},{6,14},{7,15},{8,72},{9,73... | collective-permute-start | bytes 786440 | tf_op jit(solution)/shard_map/ppermute | solution.py:18
  103.6 31.4 %slice-start = ((pred[2,2,2,64,4]{4,3,2,1,0:T(8,128)(4,1)}), pred[1,2,2,64,4]{4,3,2,1,0:T(8,128)(4,1)S(1)}, s32[]{:S(2)}) async-start(pred[2,2,2,64,4]{4,3,2,1,0:T(8,128)(4,1)} %copy-done.5), calls=%async_computation | async-start | bytes 65536 | tf_op jit(solution)/shard_map/slice | solution.py:86
  121.0 20.3 %collective-permute-start.13 = (bf16[128,512]{1,0:T(8,128)(2,1)S(1)}, bf16[128,512]{1,0:T(8,128)(2,1)S(1)}, u32[]{:S(2)}, u32[]{:S(2)}) collective-permute-start(bf16[128,512]{1,0:T(8,128)(2,1)S(1)} %fusion.11), channel_id=1, source_target_pairs={{0,256},{1,257},{2,258},{3,259},{4,260},{5,261},{6,262},{7,263},{8... | collective-permute-start | bytes 393224 | tf_op jit(solution)/shard_map/ppermute | solution.py:18
  136.0 17.0 %collective-permute-start.14 = (bf16[2,2,64,512]{3,2,1,0:T(8,128)(2,1)S(1)}, bf16[2,2,64,512]{3,2,1,0:T(8,128)(2,1)S(1)}, u32[]{:S(2)}, u32[]{:S(2)}) collective-permute-start(bf16[2,2,64,512]{3,2,1,0:T(8,128)(2,1)S(1)} %constant_dynamic-slice_fusion), channel_id=1, source_target_pairs={{0,0},{1,1},{2,32},{3,33},{4,256},{5,257},{6,288},{7,289},{8,64},{... | collective-permute-start | bytes 786440 | tf_op jit(solution)/shard_map/ppermute | solution.py:18
  141.3 61.7 %copy-start.6 = (f32[256,128]{1,0:T(8,128)S(1)}, f32[256,128]{1,0:T(8,128)}, u32[]{:S(2)}) copy-start(f32[256,128]{1,0:T(8,128)} %param.8) | copy-start | bytes 393220
  153.3 13.3 %collective-permute-start.16 = (bf16[256,128]{1,0:T(8,128)(2,1)S(1)}, bf16[256,128]{1,0:T(8,128)(2,1)S(1)}, u32[]{:S(2)}, u32[]{:S(2)}) collective-permute-start(bf16[256,128]{1,0:T(8,128)(2,1)S(1)} %bitcast.96), channel_id=1, source_target_pairs={{0,16},{1,17},{2,18},{3,19},{4,20},{5,21},{6,22},{7,23},{8,24},{9,... | collective-permute-start | bytes 196616 | tf_op jit(solution)/shard_map/ppermute | solution.py:18
  157.4 9.2 %collective-permute-start.15 = (bf16[256,128]{1,0:T(8,128)(2,1)S(1)}, bf16[256,128]{1,0:T(8,128)(2,1)S(1)}, u32[]{:S(2)}, u32[]{:S(2)}) collective-permute-start(bf16[256,128]{1,0:T(8,128)(2,1)S(1)} %bitcast.97), channel_id=1, source_target_pairs={{0,8},{1,9},{2,10},{3,11},{4,12},{5,13},{6,14},{7,15},{8,0},{9,1},... | collective-permute-start | bytes 196616 | tf_op jit(solution)/shard_map/ppermute | solution.py:18
  164.0 7.4 %collective-permute-start.17 = (bf16[256,128]{1,0:T(8,128)(2,1)S(1)}, bf16[256,128]{1,0:T(8,128)(2,1)S(1)}, u32[]{:S(2)}, u32[]{:S(2)}) collective-permute-start(bf16[256,128]{1,0:T(8,128)(2,1)S(1)} %bitcast.98), channel_id=1, source_target_pairs={{0,24},{1,25},{2,26},{3,27},{4,28},{5,29},{6,30},{7,31},{8,16},{9,... | collective-permute-start | bytes 196616 | tf_op jit(solution)/shard_map/ppermute | solution.py:18
  171.4 18.3 %collective-permute-start.18 = (bf16[256,128]{1,0:T(8,128)(2,1)S(1)}, bf16[256,128]{1,0:T(8,128)(2,1)S(1)}, u32[]{:S(2)}, u32[]{:S(2)}) collective-permute-start(bf16[256,128]{1,0:T(8,128)(2,1)S(1)} %add_convert_fusion.2), channel_id=1, source_target_pairs={{0,4},{1,5},{2,6},{3,7},{4,0},{5,1},{6,2},{7,3},{8,12},{9,13},{10,... | collective-permute-start | bytes 196616 | tf_op jit(solution)/shard_map/ppermute | solution.py:18
  189.8 7.1 %collective-permute-start.19 = (bf16[256,128]{1,0:T(8,128)(2,1)S(1)}, bf16[256,128]{1,0:T(8,128)(2,1)S(1)}, u32[]{:S(2)}, u32[]{:S(2)}) collective-permute-start(bf16[256,128]{1,0:T(8,128)(2,1)S(1)} %add_convert_fusion.1), channel_id=1, source_target_pairs={{0,2},{1,3},{2,0},{3,1},{4,6},{5,7},{6,4},{7,5},{8,10},{9,11},{10,... | collective-permute-start | bytes 196616 | tf_op jit(solution)/shard_map/ppermute | solution.py:18
  196.9 6.2 %collective-permute-start.20 = (bf16[256,128]{1,0:T(8,128)(2,1)S(1)}, bf16[256,128]{1,0:T(8,128)(2,1)S(1)}, u32[]{:S(2)}, u32[]{:S(2)}) collective-permute-start(bf16[256,128]{1,0:T(8,128)(2,1)S(1)} %add_convert_fusion), channel_id=1, source_target_pairs={{0,1},{1,0},{2,3},{3,2},{4,5},{5,4},{6,7},{7,6},{8,9},{9,8},{10,11... | collective-permute-start | bytes 196616 | tf_op jit(solution)/shard_map/ppermute | solution.py:18

commit v2 on v1

--- a/solution.py
+++ b/solution.py
@@ -27,12 +27,20 @@
     return (zl >> 2, x, (zl >> 1) & 1, (zh << 1) | (y >> 1), ((y & 1) << 2) | (core << 1) | (zl & 1))
 
 
+def swap_groups():
+    groups = []
+    for zh in range(2):
+        for core in range(2):
+            for x in range(4):
+                for zl in range(8):
+                    groups.append(
+                        [((zh * 4 + (j ^ x)) * 2 + core) * 32 + x * 8 + zl for j in range(4)]
+                    )
+    return groups
+
+
 def dot_t(left, right):
     return lax.dot_general(left, right, CONTRACT_LAST, preferred_element_type=jnp.float32)
-
-
-def flip_if(value, bit, axis):
-    return jnp.where(bit == 0, value, jnp.flip(value, axis))
 
 
 def per_device(ainv, lpanel, dinv, rowblocks, counts, widths):
@@ -56,7 +64,8 @@
         send(a3[:half], lambda zh, y, core, x, zl: (zh, y, core, x ^ 1, zl)),
         send(a1[half:], lambda zh, y, core, x, zl: (zh, y, core, x ^ 3, zl)),
     ]
-    a2 = jnp.concatenate(a2, axis=0)
+    last, upper, lower = lax.optimization_barrier((last, *a2))
+    a2 = jnp.concatenate([upper, lower], axis=0)
 
     slots = jnp.arange(rowblocks.shape[1], dtype=jnp.int32)
     used = jnp.where(slots[None, :] < counts[:, None], rowblocks, -1)
@@ -70,21 +79,18 @@
         chosen[:, None, :, None] & block_is[None, :, None, :] & member[None, None, :, :], axis=(2, 3)
     )
     width = jnp.sum(jnp.where(chosen, widths[None, :], 0), axis=1)
-    quarter = (
-        (mid ^ jnp.arange(2, dtype=jnp.int32))[:, None] * 2
-        + (low ^ jnp.arange(2, dtype=jnp.int32))[None, :]
-    )
-    within = quarter[:, :, None] * 64 + jnp.arange(64, dtype=jnp.int32)[None, None, :]
+    half_of = (mid ^ jnp.arange(2, dtype=jnp.int32))[:, None, None] * 128
+    within = half_of + jnp.arange(128, dtype=jnp.int32).reshape(1, 2, 64)
     active = within[None] < width[:, None, None, None]
 
-    factor = jnp.stack([quad, last], axis=2)
-    keep_mask = active[..., None, None] & live[:, None, None, None, :, None]
-    factor = jnp.where(
-        keep_mask, factor.reshape(2, 2, 2, 64, 4, B), jnp.zeros((), jnp.bfloat16)
-    ).reshape(2, 2, 2, 64, 1024)
+    factor = jnp.stack(
+        [jnp.where(low == 0, quad, last), jnp.where(low == 0, last, quad)], axis=2
+    )
+    row_scale = jnp.repeat(live.astype(jnp.bfloat16), B, axis=1)
+    factor = factor * active[..., None].astype(jnp.bfloat16) * row_scale[:, None, None, None, :]
 
-    mine = lax.dynamic_slice_in_dim(factor[0], low * 512, 512, axis=3)
-    across = send(mine, rows_home)
+    mine = lax.dynamic_slice_in_dim(factor[0, 0].reshape(128, 1024), low * 512, 512, axis=1)
+    mine = send(mine, rows_home)
 
     keep = core ^ mid
     theirs = lax.dynamic_index_in_dim(factor, 1 - keep, 1, keepdims=False).reshape(256, 1024)
@@ -95,18 +101,23 @@
     here = jnp.stack([dot_t(ours, block) for block in blocks])
     chip = (here + other.astype(jnp.float32)).astype(jnp.bfloat16)
 
-    total = None
-    for k in range(4):
-        share = lax.dynamic_index_in_dim(chip, y ^ k ^ x, 0, keepdims=False)
-        came = send(share, lambda zh, y, core, x, zl: (zh, x, core, y ^ k, zl)).astype(jnp.float32)
-        total = came if total is None else total + came
-    total = total.reshape(2, 128, 512)
+    chip, mine = lax.optimization_barrier((chip, mine))
+    shares = lax.all_to_all(chip, AXES, 0, 0, axis_index_groups=swap_groups())
+    beside = send(mine, lambda zh, y, core, x, zl: (zh, y, core ^ 1, x, zl))
+    across = jnp.concatenate([jnp.where(core == 0, mine, beside), jnp.where(core == 0, beside, mine)])
+    rounded = jnp.sum(shares.astype(jnp.float32), axis=0).reshape(2, 128, 512).astype(jnp.bfloat16)
 
     stay = zh ^ high
-    leave = lax.dynamic_index_in_dim(total, 1 - stay, 0, keepdims=False).astype(jnp.bfloat16)
-    came = send(leave, lambda zh, y, core, x, zl: (zh ^ 1, y, core, x, zl))
-    product = lax.dynamic_index_in_dim(total, stay, 0, keepdims=False) + came.astype(jnp.float32)
-    product = flip_if(product.reshape(2, 64, 512), low, 0).reshape(128, 512)
+    part = [lax.dynamic_index_in_dim(rounded, stay ^ k, 0, keepdims=False) for k in range(2)]
+    far = send(part[1], lambda zh, y, core, x, zl: (zh ^ 1, x, core, y, zl))
+    near = send(part[0], lambda zh, y, core, x, zl: (zh, x, core, y, zl))
+    product = near.astype(jnp.float32) + far.astype(jnp.float32)
+
+    terms = dot_t(across, product.astype(jnp.bfloat16)).astype(jnp.bfloat16)
+    pieces = lax.all_to_all(terms.reshape(32, 8, 128), "pcol", 0, 0)
+    piece = jnp.sum(pieces.astype(jnp.float32), axis=0).astype(jnp.bfloat16)
+    terms = lax.all_to_all(jnp.broadcast_to(piece[None], (32, 8, 128)), "pcol", 0, 0)
+    terms = terms.reshape(256, 128).astype(jnp.float32)
 
     node = prow >> 1
     row_ids = pcol * 2 + jnp.arange(2, dtype=jnp.int32)
@@ -118,19 +129,6 @@
     )
     negated = jnp.where(kept[None, :, None], -product.reshape(128, 2, B), 0.0).reshape(128, 512)
     selected_inverse = negated.astype(jnp.bfloat16).T
-
-    terms = dot_t(across.reshape(256, 512), product.astype(jnp.bfloat16))
-    terms = flip_if(flip_if(terms.reshape(2, 2, 64, 128), low, 1), core, 0).reshape(256, 128)
-    terms = terms.astype(jnp.bfloat16)
-    by_x = [terms] + [
-        send(terms, lambda zh, y, core, x, zl: (zh, y, core, x ^ k, zl)) for k in (1, 2, 3)
-    ]
-    by_x = [part.astype(jnp.float32) for part in by_x]
-    terms = (by_x[0] + by_x[1]) + (by_x[2] + by_x[3])
-    for bit in (4, 2, 1):
-        sent = terms.astype(jnp.bfloat16)
-        came = send(sent, lambda zh, y, core, x, zl: (zh, y, core, x, zl ^ bit))
-        terms = sent.astype(jnp.float32) + came.astype(jnp.float32)
 
     my_width = jnp.sum(jnp.where(nodes == node, widths, 0))
     column = core * 128 + jnp.arange(128, dtype=jnp.int32)

time: 206 us -> 185 us (0.90)
  starting transfers between devices: 98 us -> 90 us
  waiting for transfers between devices: 78.6 us -> 72.7 us
  local copies, waits for them, and re-layouts: 9.05 us -> 4.38 us
    ppermute x21 -> x13, waiting for transfers between devices: 78.6 us -> 39.2 us  [send(): return lax.ppermute(value, AXES, pairs)]
    all_to_all x0 -> x3, waiting for transfers between devices: none -> 33.5 us  [the longest x1 11.8 us: per_device(): pieces = lax.all_to_all(terms.reshape(32, 8, 128), 'pcol', 0, 0)]
    ppermute x21 -> x13, starting transfers between devices: 98 us -> 65.7 us  [send(): return lax.ppermute(value, AXES, pairs)]
    all_to_all x0 -> x3, starting transfers between devices: none -> 24.3 us  [the longest x1 15.9 us: per_device(): pieces = lax.all_to_all(terms.reshape(32, 8, 128), 'pcol', 0, 0)]
    broadcast_in_dim x2 -> x1, local copies, waits for them, and re-layouts: 4.33 us -> 0.64 us  [per_device(): jnp.broadcast_to(piece[None], (32, 8, 128))]
  transfers between devices with their start and end apart: 21 -> 16, of which waited for: 12 -> 9; matrix products, arithmetic and copies ran while one was open for 9% -> 7% of each run, Pallas kernels for 0% -> 0%
where the time goes in v2:
time: 185 us; the launch traced here: 184 us
  starting transfers between devices  90 us (49%)
  waiting for transfers between devices  72.7 us (39%)
  other arithmetic  9.75 us (5%)
  matrix products  6.01 us (3%)
  local copies, waits for them, and re-layouts  4.38 us (2%)
    ppermute x13, starting transfers between devices, send(): return lax.ppermute(value, AXES, pairs)  65.7 us
    ppermute x13, waiting for transfers between devices, send(): return lax.ppermute(value, AXES, pairs)  39.2 us
    all_to_all x1, starting transfers between devices, per_device(): pieces = lax.all_to_all(terms.reshape(32, 8, 128), 'pcol', 0, 0)  15.9 us
    all_to_all x1, waiting for transfers between devices, per_device(): pieces = lax.all_to_all(terms.reshape(32, 8, 128), 'pcol', 0, 0)  11.8 us
    all_to_all x1, waiting for transfers between devices, per_device(): lax.all_to_all(jnp.broadcast_to(piece[None], (32, 8, 128)), 'pcol', 0, 0)  11.1 us
    all_to_all x1, waiting for transfers between devices, per_device(): shares = lax.all_to_all(chip, AXES, 0, 0, axis_index_groups=swap_groups())  10.7 us
    dot_general x9, matrix products, dot_t(): lax.dot_general(left, right, CONTRACT_LAST, preferred_element_type=jnp.fl...  6.01 us
    all_to_all x1, starting transfers between devices, per_device(): shares = lax.all_to_all(chip, AXES, 0, 0, axis_index_groups=swap_groups())  4.5 us
  transfers between devices with their start and end apart: 16, of which 9 were waited for; matrix products, arithmetic and copies ran while one was open for 7% of the time, Pallas kernels for 0%

profile of v2, /device:TPU:24, one launch (start us, length us, event | category | flops | bytes accessed | tf_op | source)
XLA Modules:
  0.0 183.9 jit_solution(17475900427764329971)
XLA Ops:
  0.6 9.1 %collective-permute-start.1 = (bf16[64,1024]{1,0:T(8,128)(2,1)}, bf16[64,1024]{1,0:T(8,128)(2,1)S(1)}, u32[]{:S(2)}, u32[]{:S(2)}) collective-permute-start(bf16[64,1024]{1,0:T(8,128)(2,1)} %bitcast.77), channel_id=1, source_target_pairs={{0,4},{1,5},{2,6},{3,7},{4,12},{5,13},{6,14},{7,15},{8,20},{9,21},... | collective-permute-start | bytes 393224 | tf_op jit(solution)/shard_map/ppermute | solution.py:18
  9.7 1.6 collective-permute-start
  11.3 4.7 %collective-permute-start.6 = (bf16[512,1024]{1,0:T(8,128)(2,1)}, bf16[512,1024]{1,0:T(8,128)(2,1)S(1)}, u32[]{:S(2)}, u32[]{:S(2)}) collective-permute-start(bf16[512,1024]{1,0:T(8,128)(2,1)} %param.6), channel_id=1, source_target_pairs={{0,8},{1,9},{2,10},{3,11},{4,12},{5,13},{6,14},{7,15},{8,0},{9,1},... | collective-permute-start | bytes 3145736 | tf_op jit(solution)/shard_map/ppermute | solution.py:18
  16.0 4.5 %collective-permute-start.4 = (bf16[512,1024]{1,0:T(8,128)(2,1)}, bf16[512,1024]{1,0:T(8,128)(2,1)S(1)}, u32[]{:S(2)}, u32[]{:S(2)}) collective-permute-start(bf16[512,1024]{1,0:T(8,128)(2,1)} %param.6), channel_id=1, source_target_pairs={{0,24},{1,25},{2,26},{3,27},{4,28},{5,29},{6,30},{7,31},{8,16},{9,... | collective-permute-start | bytes 3145736 | tf_op jit(solution)/shard_map/ppermute | solution.py:18
  22.0 5.2 %collective-permute-start.2 = (bf16[2,64,1024]{2,1,0:T(8,128)(2,1)S(1)}, bf16[2,64,1024]{2,1,0:T(8,128)(2,1)S(1)}, u32[]{:S(2)}, u32[]{:S(2)}) collective-permute-start(bf16[2,64,1024]{2,1,0:T(8,128)(2,1)S(1)} %get-tuple-element.25), channel_id=1, source_target_pairs={{0,2},{1,3},{2,0},{3,1},{4,6},{5,7},{6,4},{7,5},{8,10},{9,11},{10,... | collective-permute-start | bytes 786440 | tf_op jit(solution)/shard_map/ppermute | solution.py:18
  27.2 0.8 select_reduce_fusion
  28.1 12.6 %collective-permute-done.2 = bf16[2,64,1024]{2,1,0:T(8,128)(2,1)S(1)} collective-permute-done((bf16[2,64,1024]{2,1,0:T(8,128)(2,1)S(1)}, bf16[2,64,1024]{2,1,0:T(8,128)(2,1)S(1)}, u32[]{:S(2)}, u32[]{:S(2)}) %collective-permute-start.2) | collective-permute-done | bytes 262176 | tf_op jit(solution)/shard_map/ppermute | solution.py:18
  40.7 1.9 %collective-permute-start.3 = (bf16[2,2,64,1024]{3,2,0,1:T(8,128)(2,1)S(1)}, bf16[2,2,64,1024]{3,2,0,1:T(8,128)(2,1)S(1)}, u32[]{:S(2)}, u32[]{:S(2)}) collective-permute-start(bf16[2,2,64,1024]{3,2,0,1:T(8,128)(2,1)S(1)} %pad_maximum_fusion.1), channel_id=1, source_target_pairs={{0,1},{1,0},{2,3},{3,2},{4,5},{5,4},{6,7},{7,6},{8,9},{9,8},{10,11... | collective-permute-start | bytes 1572872 | tf_op jit(solution)/shard_map/ppermute | solution.py:18
  42.7 4.7 %collective-permute-start.7 = (bf16[256,1024]{1,0:T(8,128)(2,1)S(1)}, bf16[256,1024]{1,0:T(8,128)(2,1)S(1)}, u32[]{:S(2)}, u32[]{:S(2)}) collective-permute-start(bf16[256,1024]{1,0:T(8,128)(2,1)S(1)} %slice.13), channel_id=1, source_target_pairs={{0,24},{1,25},{2,26},{3,27},{4,28},{5,29},{6,30},{7,31},{8,16},{9,... | collective-permute-start | bytes 1572872 | tf_op jit(solution)/shard_map/ppermute | solution.py:18
  47.5 2.0 %collective-permute-start.5 = (bf16[256,1024]{1,0:T(8,128)(2,1)S(1)}, bf16[256,1024]{1,0:T(8,128)(2,1)S(1)}, u32[]{:S(2)}, u32[]{:S(2)}) collective-permute-start(bf16[256,1024]{1,0:T(8,128)(2,1)S(1)} %slice.12), channel_id=1, source_target_pairs={{0,8},{1,9},{2,10},{3,11},{4,12},{5,13},{6,14},{7,15},{8,0},{9,1},... | collective-permute-start | bytes 1572872 | tf_op jit(solution)/shard_map/ppermute | solution.py:18
  49.6 5.2 %collective-permute-done.3 = bf16[2,2,64,1024]{3,2,0,1:T(8,128)(2,1)S(1)} collective-permute-done((bf16[2,2,64,1024]{3,2,0,1:T(8,128)(2,1)S(1)}, bf16[2,2,64,1024]{3,2,0,1:T(8,128)(2,1)S(1)}, u32[]{:S(2)}, u32[]{:S(2)}) %collective-permute-start.3) | collective-permute-done | bytes 524320 | tf_op jit(solution)/shard_map/ppermute | solution.py:18
  54.8 4.7 %collective-permute-done.7 = bf16[256,1024]{1,0:T(8,128)(2,1)S(1)} collective-permute-done((bf16[256,1024]{1,0:T(8,128)(2,1)S(1)}, bf16[256,1024]{1,0:T(8,128)(2,1)S(1)}, u32[]{:S(2)}, u32[]{:S(2)}) %collective-permute-start.7) | collective-permute-done | bytes 524320 | tf_op jit(solution)/shard_map/ppermute | solution.py:18
  59.5 3.4 %collective-permute-done.5 = bf16[256,1024]{1,0:T(8,128)(2,1)S(1)} collective-permute-done((bf16[256,1024]{1,0:T(8,128)(2,1)S(1)}, bf16[256,1024]{1,0:T(8,128)(2,1)S(1)}, u32[]{:S(2)}, u32[]{:S(2)}) %collective-permute-start.5) | collective-permute-done | bytes 524320 | tf_op jit(solution)/shard_map/ppermute | solution.py:18
  63.3 0.9 copy-done.2
  66.9 1.1 pad_maximum_fusion
  68.0 1.9 %collective-permute-start.8 = (bf16[4,256,512]{2,1,0:T(8,128)(2,1)}, bf16[4,256,512]{2,1,0:T(8,128)(2,1)}, u32[]{:S(2)}, u32[]{:S(2)}) collective-permute-start(bf16[4,256,512]{2,1,0:T(8,128)(2,1)} %pad_maximum_fusion), channel_id=1, source_target_pairs={{0,32},{1,33},{2,34},{3,35},{4,36},{5,37},{6,38},{7,39},{8,40},{9,... | collective-permute-start | bytes 3145736 | tf_op jit(solution)/shard_map/ppermute | solution.py:18
  69.9 1.0 slice.14
  70.9 5.2 %collective-permute-start.9 = (bf16[128,512]{1,0:T(8,128)(2,1)S(1)}, bf16[128,512]{1,0:T(8,128)(2,1)S(1)}, u32[]{:S(2)}, u32[]{:S(2)}) collective-permute-start(bf16[128,512]{1,0:T(8,128)(2,1)S(1)} %constant_dynamic-slice_fusion), channel_id=1, source_target_pairs={{0,0},{1,1},{2,32},{3,33},{4,256},{5,257},{6,288},{7,289},{8,64},{... | collective-permute-start | bytes 393224 | tf_op jit(solution)/shard_map/ppermute | solution.py:18
  76.1 1.8 convolution_bitcast_fusion.3
  79.4 2.6 %fusion = bf16[4,256,512]{2,1,0:T(8,128)(2,1)} fusion(f32[1,256,512]{2,1,0:T(8,128)S(1)} %convolution_bitcast_fusion, f32[1,256,512]{2,1,0:T(8,128)S(1)} %convolution_bitcast_fusion.1, f32[1,256,512]{2,1,0:T(8,128)S(1)} %convolution_bitcast_fusion.2, f32[1,256,512]{2,1,0:T(8,128)S(1)} %convolution_bitcast_fusion.3, bf16[4,256,512]{2,1,0:T(8,128)(2,1)} %collective-permute-done.8), kind=kLoop, calls=%fused_computation.1 | loop fusion | flops 3145728 | bytes 4194304 | tf_op jit(solution)/shard_map/convert_element_type | solution.py:102
  82.0 3.3 %collective-permute-done.9 = bf16[128,512]{1,0:T(8,128)(2,1)S(1)} collective-permute-done((bf16[128,512]{1,0:T(8,128)(2,1)S(1)}, bf16[128,512]{1,0:T(8,128)(2,1)S(1)}, u32[]{:S(2)}, u32[]{:S(2)}) %collective-permute-start.9) | collective-permute-done | bytes 131104 | tf_op jit(solution)/shard_map/ppermute | solution.py:18
  85.3 4.5 %all-to-all-start = ((bf16[4,256,512]{2,1,0:T(8,128)(2,1)}), bf16[4,256,512]{2,1,0:T(8,128)(2,1)S(1)}, u32[]{:S(2)}, u32[]{:S(2)}) async-start(bf16[4,256,512]{2,1,0:T(8,128)(2,1)} %fusion), calls=%async_computation | async-start | bytes 2097152 | tf_op jit(solution)/shard_map/all_to_all | solution.py:105
  89.9 1.9 %collective-permute-start.12 = (bf16[128,512]{1,0:T(8,128)(2,1)S(1)}, bf16[128,512]{1,0:T(8,128)(2,1)S(1)}, u32[]{:S(2)}, u32[]{:S(2)}) collective-permute-start(bf16[128,512]{1,0:T(8,128)(2,1)S(1)} %collective-permute-done.9), channel_id=1, source_target_pairs={{0,32},{1,33},{2,34},{3,35},{4,36},{5,37},{6,38},{7,39},{8,40},{9,... | collective-permute-start | bytes 393224 | tf_op jit(solution)/shard_map/ppermute | solution.py:18
  92.5 10.7 %all-to-all-done = bf16[4,256,512]{2,1,0:T(8,128)(2,1)S(1)} async-done(((bf16[4,256,512]{2,1,0:T(8,128)(2,1)}), bf16[4,256,512]{2,1,0:T(8,128)(2,1)S(1)}, u32[]{:S(2)}, u32[]{:S(2)}) %all-to-all-start) | async-done | bytes 1048608 | tf_op jit(solution)/shard_map/all_to_all | solution.py:105
  103.4 8.3 %collective-permute-start.10 = (bf16[128,512]{1,0:T(8,128)(2,1)S(1)}, bf16[128,512]{1,0:T(8,128)(2,1)S(1)}, u32[]{:S(2)}, u32[]{:S(2)}) collective-permute-start(bf16[128,512]{1,0:T(8,128)(2,1)S(1)} %get-tuple-element.22), channel_id=1, source_target_pairs={{0,0},{1,1},{2,2},{3,3},{4,4},{5,5},{6,6},{7,7},{8,64},{9,65},{10,... | collective-permute-start | bytes 393224 | tf_op jit(solution)/shard_map/ppermute | solution.py:18
  111.7 14.8 %collective-permute-start.11 = (bf16[128,512]{1,0:T(8,128)(2,1)S(1)}, bf16[128,512]{1,0:T(8,128)(2,1)S(1)}, u32[]{:S(2)}, u32[]{:S(2)}) collective-permute-start(bf16[128,512]{1,0:T(8,128)(2,1)S(1)} %get-tuple-element.23), channel_id=1, source_target_pairs={{0,256},{1,257},{2,258},{3,259},{4,260},{5,261},{6,262},{7,263},{8... | collective-permute-start | bytes 393224 | tf_op jit(solution)/shard_map/ppermute | solution.py:18
  126.6 9.9 %collective-permute-done.11 = bf16[128,512]{1,0:T(8,128)(2,1)S(1)} collective-permute-done((bf16[128,512]{1,0:T(8,128)(2,1)S(1)}, bf16[128,512]{1,0:T(8,128)(2,1)S(1)}, u32[]{:S(2)}, u32[]{:S(2)}) %collective-permute-start.11) | collective-permute-done | bytes 131104 | tf_op jit(solution)/shard_map/ppermute | solution.py:18
  136.5 0.9 fusion.5
  137.4 15.9 %all-to-all-start.1 = ((bf16[32,8,128]{2,1,0:T(8,128)(2,1)}), bf16[32,8,128]{2,1,0:T(8,128)(2,1)S(1)}, u32[]{:S(2)}, u32[]{:S(2)}) async-start(bf16[32,8,128]{2,1,0:T(8,128)(2,1)} %fusion.5), calls=%async_computation.1 | async-start | bytes 131072 | tf_op jit(solution)/shard_map/all_to_all | solution.py:117
  154.1 11.8 %all-to-all-done.1 = bf16[32,8,128]{2,1,0:T(8,128)(2,1)S(1)} async-done(((bf16[32,8,128]{2,1,0:T(8,128)(2,1)}), bf16[32,8,128]{2,1,0:T(8,128)(2,1)S(1)}, u32[]{:S(2)}, u32[]{:S(2)}) %all-to-all-start.1) | async-done | bytes 65568 | tf_op jit(solution)/shard_map/all_to_all | solution.py:117
  166.6 3.9 %all-to-all-start.2 = ((bf16[32,8,128]{2,1,0:T(8,128)(2,1)}), bf16[32,8,128]{2,1,0:T(8,128)(2,1)S(1)}, u32[]{:S(2)}, u32[]{:S(2)}) async-start(bf16[32,8,128]{2,1,0:T(8,128)(2,1)} %broadcast_in_dim.83), calls=%async_computation.2 | async-start | bytes 131072 | tf_op jit(solution)/shard_map/all_to_all | solution.py:119
  172.0 11.1 %all-to-all-done.2 = bf16[32,8,128]{2,1,0:T(8,128)(2,1)S(1)} async-done(((bf16[32,8,128]{2,1,0:T(8,128)(2,1)}), bf16[32,8,128]{2,1,0:T(8,128)(2,1)S(1)}, u32[]{:S(2)}, u32[]{:S(2)}) %all-to-all-start.2) | async-done | bytes 65568 | tf_op jit(solution)/shard_map/all_to_all | solution.py:119
  (66 shorter events, 11.1 us)
Async XLA Ops:
  0.6 21.3 %collective-permute-start.1 = (bf16[64,1024]{1,0:T(8,128)(2,1)}, bf16[64,1024]{1,0:T(8,128)(2,1)S(1)}, u32[]{:S(2)}, u32[]{:S(2)}) collective-permute-start(bf16[64,1024]{1,0:T(8,128)(2,1)} %bitcast.77), channel_id=1, source_target_pairs={{0,4},{1,5},{2,6},{3,7},{4,12},{5,13},{6,14},{7,15},{8,20},{9,21},... | collective-permute-start | bytes 393224 | tf_op jit(solution)/shard_map/ppermute | solution.py:18
  9.7 12.2 %collective-permute-start = (bf16[64,1024]{1,0:T(8,128)(2,1)}, bf16[64,1024]{1,0:T(8,128)(2,1)S(1)}, u32[]{:S(2)}, u32[]{:S(2)}) collective-permute-start(bf16[64,1024]{1,0:T(8,128)(2,1)} %bitcast.78), channel_id=1, source_target_pairs={{0,0},{1,1},{2,2},{3,3},{4,8},{5,9},{6,10},{7,11},{8,16},{9,17},{1... | collective-permute-start | bytes 393224 | tf_op jit(solution)/shard_map/ppermute | solution.py:18
  11.3 31.4 %collective-permute-start.6 = (bf16[512,1024]{1,0:T(8,128)(2,1)}, bf16[512,1024]{1,0:T(8,128)(2,1)S(1)}, u32[]{:S(2)}, u32[]{:S(2)}) collective-permute-start(bf16[512,1024]{1,0:T(8,128)(2,1)} %param.6), channel_id=1, source_target_pairs={{0,8},{1,9},{2,10},{3,11},{4,12},{5,13},{6,14},{7,15},{8,0},{9,1},... | collective-permute-start | bytes 3145736 | tf_op jit(solution)/shard_map/ppermute | solution.py:18
  16.0 31.4 %collective-permute-start.4 = (bf16[512,1024]{1,0:T(8,128)(2,1)}, bf16[512,1024]{1,0:T(8,128)(2,1)S(1)}, u32[]{:S(2)}, u32[]{:S(2)}) collective-permute-start(bf16[512,1024]{1,0:T(8,128)(2,1)} %param.6), channel_id=1, source_target_pairs={{0,24},{1,25},{2,26},{3,27},{4,28},{5,29},{6,30},{7,31},{8,16},{9,... | collective-permute-start | bytes 3145736 | tf_op jit(solution)/shard_map/ppermute | solution.py:18
  22.0 18.7 %collective-permute-start.2 = (bf16[2,64,1024]{2,1,0:T(8,128)(2,1)S(1)}, bf16[2,64,1024]{2,1,0:T(8,128)(2,1)S(1)}, u32[]{:S(2)}, u32[]{:S(2)}) collective-permute-start(bf16[2,64,1024]{2,1,0:T(8,128)(2,1)S(1)} %get-tuple-element.25), channel_id=1, source_target_pairs={{0,2},{1,3},{2,0},{3,1},{4,6},{5,7},{6,4},{7,5},{8,10},{9,11},{10,... | collective-permute-start | bytes 786440 | tf_op jit(solution)/shard_map/ppermute | solution.py:18
  40.7 14.1 %collective-permute-start.3 = (bf16[2,2,64,1024]{3,2,0,1:T(8,128)(2,1)S(1)}, bf16[2,2,64,1024]{3,2,0,1:T(8,128)(2,1)S(1)}, u32[]{:S(2)}, u32[]{:S(2)}) collective-permute-start(bf16[2,2,64,1024]{3,2,0,1:T(8,128)(2,1)S(1)} %pad_maximum_fusion.1), channel_id=1, source_target_pairs={{0,1},{1,0},{2,3},{3,2},{4,5},{5,4},{6,7},{7,6},{8,9},{9,8},{10,11... | collective-permute-start | bytes 1572872 | tf_op jit(solution)/shard_map/ppermute | solution.py:18
  42.7 16.8 %collective-permute-start.7 = (bf16[256,1024]{1,0:T(8,128)(2,1)S(1)}, bf16[256,1024]{1,0:T(8,128)(2,1)S(1)}, u32[]{:S(2)}, u32[]{:S(2)}) collective-permute-start(bf16[256,1024]{1,0:T(8,128)(2,1)S(1)} %slice.13), channel_id=1, source_target_pairs={{0,24},{1,25},{2,26},{3,27},{4,28},{5,29},{6,30},{7,31},{8,16},{9,... | collective-permute-start | bytes 1572872 | tf_op jit(solution)/shard_map/ppermute | solution.py:18
  47.5 15.5 %collective-permute-start.5 = (bf16[256,1024]{1,0:T(8,128)(2,1)S(1)}, bf16[256,1024]{1,0:T(8,128)(2,1)S(1)}, u32[]{:S(2)}, u32[]{:S(2)}) collective-permute-start(bf16[256,1024]{1,0:T(8,128)(2,1)S(1)} %slice.12), channel_id=1, source_target_pairs={{0,8},{1,9},{2,10},{3,11},{4,12},{5,13},{6,14},{7,15},{8,0},{9,1},... | collective-permute-start | bytes 1572872 | tf_op jit(solution)/shard_map/ppermute | solution.py:18
  63.2 1.0 copy-start.2
  63.2 1.6 copy-start.3
  65.4 1.0 copy-start
  68.0 11.4 %collective-permute-start.8 = (bf16[4,256,512]{2,1,0:T(8,128)(2,1)}, bf16[4,256,512]{2,1,0:T(8,128)(2,1)}, u32[]{:S(2)}, u32[]{:S(2)}) collective-permute-start(bf16[4,256,512]{2,1,0:T(8,128)(2,1)} %pad_maximum_fusion), channel_id=1, source_target_pairs={{0,32},{1,33},{2,34},{3,35},{4,36},{5,37},{6,38},{7,39},{8,40},{9,... | collective-permute-start | bytes 3145736 | tf_op jit(solution)/shard_map/ppermute | solution.py:18
  70.9 14.4 %collective-permute-start.9 = (bf16[128,512]{1,0:T(8,128)(2,1)S(1)}, bf16[128,512]{1,0:T(8,128)(2,1)S(1)}, u32[]{:S(2)}, u32[]{:S(2)}) collective-permute-start(bf16[128,512]{1,0:T(8,128)(2,1)S(1)} %constant_dynamic-slice_fusion), channel_id=1, source_target_pairs={{0,0},{1,1},{2,32},{3,33},{4,256},{5,257},{6,288},{7,289},{8,64},{... | collective-permute-start | bytes 393224 | tf_op jit(solution)/shard_map/ppermute | solution.py:18
  76.1 1.8 copy-start.1
  82.0 9.8 %copy-start.5 = (s32[8]{0:T(128)S(1)}, s32[8]{0:T(128)}, u32[]{:S(2)}) copy-start(s32[8]{0:T(128)} %param.11) | copy-start | bytes 100
  85.3 17.8 %all-to-all-start = ((bf16[4,256,512]{2,1,0:T(8,128)(2,1)}), bf16[4,256,512]{2,1,0:T(8,128)(2,1)S(1)}, u32[]{:S(2)}, u32[]{:S(2)}) async-start(bf16[4,256,512]{2,1,0:T(8,128)(2,1)} %fusion), calls=%async_computation | async-start | bytes 2097152 | tf_op jit(solution)/shard_map/all_to_all | solution.py:105
  89.9 36.6 %collective-permute-start.12 = (bf16[128,512]{1,0:T(8,128)(2,1)S(1)}, bf16[128,512]{1,0:T(8,128)(2,1)S(1)}, u32[]{:S(2)}, u32[]{:S(2)}) collective-permute-start(bf16[128,512]{1,0:T(8,128)(2,1)S(1)} %collective-permute-done.9), channel_id=1, source_target_pairs={{0,32},{1,33},{2,34},{3,35},{4,36},{5,37},{6,38},{7,39},{8,40},{9,... | collective-permute-start | bytes 393224 | tf_op jit(solution)/shard_map/ppermute | solution.py:18
  103.4 23.2 %collective-permute-start.10 = (bf16[128,512]{1,0:T(8,128)(2,1)S(1)}, bf16[128,512]{1,0:T(8,128)(2,1)S(1)}, u32[]{:S(2)}, u32[]{:S(2)}) collective-permute-start(bf16[128,512]{1,0:T(8,128)(2,1)S(1)} %get-tuple-element.22), channel_id=1, source_target_pairs={{0,0},{1,1},{2,2},{3,3},{4,4},{5,5},{6,6},{7,7},{8,64},{9,65},{10,... | collective-permute-start | bytes 393224 | tf_op jit(solution)/shard_map/ppermute | solution.py:18
  111.7 71.4 %copy-start.4 = (f32[256,128]{1,0:T(8,128)S(1)}, f32[256,128]{1,0:T(8,128)}, u32[]{:S(2)}) copy-start(f32[256,128]{1,0:T(8,128)} %param.8) | copy-start | bytes 393220
  111.7 24.8 %collective-permute-start.11 = (bf16[128,512]{1,0:T(8,128)(2,1)S(1)}, bf16[128,512]{1,0:T(8,128)(2,1)S(1)}, u32[]{:S(2)}, u32[]{:S(2)}) collective-permute-start(bf16[128,512]{1,0:T(8,128)(2,1)S(1)} %get-tuple-element.23), channel_id=1, source_target_pairs={{0,256},{1,257},{2,258},{3,259},{4,260},{5,261},{6,262},{7,263},{8... | collective-permute-start | bytes 393224 | tf_op jit(solution)/shard_map/ppermute | solution.py:18
  137.4 28.5 %all-to-all-start.1 = ((bf16[32,8,128]{2,1,0:T(8,128)(2,1)}), bf16[32,8,128]{2,1,0:T(8,128)(2,1)S(1)}, u32[]{:S(2)}, u32[]{:S(2)}) async-start(bf16[32,8,128]{2,1,0:T(8,128)(2,1)} %fusion.5), calls=%async_computation.1 | async-start | bytes 131072 | tf_op jit(solution)/shard_map/all_to_all | solution.py:117
  166.6 16.6 %all-to-all-start.2 = ((bf16[32,8,128]{2,1,0:T(8,128)(2,1)}), bf16[32,8,128]{2,1,0:T(8,128)(2,1)S(1)}, u32[]{:S(2)}, u32[]{:S(2)}) async-start(bf16[32,8,128]{2,1,0:T(8,128)(2,1)} %broadcast_in_dim.83), calls=%async_computation.2 | async-start | bytes 131072 | tf_op jit(solution)/shard_map/all_to_all | solution.py:119

commit v3 on v2

--- a/solution.py
+++ b/solution.py
@@ -1,6 +1,10 @@
+import functools
+
 import jax
 import jax.numpy as jnp
 from jax import lax
+from jax.experimental import pallas as pl
+from jax.experimental.pallas import tpu as pltpu
 from jax.sharding import PartitionSpec as P
 
 B = 256
@@ -43,6 +47,38 @@
     return lax.dot_general(left, right, CONTRACT_LAST, preferred_element_type=jnp.float32)
 
 
+def product_kernel(added, factor, near, one, upper, lower, three, *rest):
+    out = rest[-1]
+    half = upper.shape[0]
+    for place, rows in ((0, near), (1, one), (3, three)):
+        term = dot_t(factor[...], rows[...])
+        if added:
+            term = term + rest[0][place].astype(jnp.float32)
+        out[place] = term.astype(jnp.bfloat16)
+    for columns, rows in ((slice(0, half), upper), (slice(half, 2 * half), lower)):
+        term = dot_t(factor[...], rows[...])
+        if added:
+            term = term + rest[0][2, :, columns].astype(jnp.float32)
+        out[2, :, columns] = term.astype(jnp.bfloat16)
+
+
+def partial_product(factor, blocks, *added):
+    width, depth = factor.shape
+    height = blocks[0].shape[0]
+    return pl.pallas_call(
+        functools.partial(product_kernel, len(added)),
+        in_specs=[pl.BlockSpec(memory_space=pltpu.VMEM)] * (6 + len(added)),
+        out_specs=pl.BlockSpec(memory_space=pltpu.VMEM),
+        out_shape=jax.ShapeDtypeStruct((4, width, height), jnp.bfloat16),
+        cost_estimate=pl.CostEstimate(
+            flops=8 * width * height * depth,
+            bytes_accessed=8 * height * depth + 2 * width * depth + 8 * width * height,
+            transcendentals=0,
+        ),
+        compiler_params=pltpu.CompilerParams(vmem_limit_bytes=12 * 1024 * 1024),
+    )(factor, *blocks, *added)
+
+
 def per_device(ainv, lpanel, dinv, rowblocks, counts, widths):
     prow, pcol = lax.axis_index("prow"), lax.axis_index("pcol")
     zh, y, core = prow >> 3, (prow >> 1) & 3, prow & 1
@@ -64,8 +100,6 @@
         send(a3[:half], lambda zh, y, core, x, zl: (zh, y, core, x ^ 1, zl)),
         send(a1[half:], lambda zh, y, core, x, zl: (zh, y, core, x ^ 3, zl)),
     ]
-    last, upper, lower = lax.optimization_barrier((last, *a2))
-    a2 = jnp.concatenate([upper, lower], axis=0)
 
     slots = jnp.arange(rowblocks.shape[1], dtype=jnp.int32)
     used = jnp.where(slots[None, :] < counts[:, None], rowblocks, -1)
@@ -95,13 +129,12 @@
     keep = core ^ mid
     theirs = lax.dynamic_index_in_dim(factor, 1 - keep, 1, keepdims=False).reshape(256, 1024)
     ours = lax.dynamic_index_in_dim(factor, keep, 1, keepdims=False).reshape(256, 1024)
-    blocks = [ainv, a1, a2, a3]
-    away = jnp.stack([dot_t(theirs, block).astype(jnp.bfloat16) for block in blocks])
+    ours, theirs, upper, lower = lax.optimization_barrier((ours, theirs, *a2))
+    blocks = (ainv, a1, upper, lower, a3)
+    away, mine = lax.optimization_barrier((partial_product(theirs, blocks), mine))
     other = send(away, lambda zh, y, core, x, zl: (zh, y, core ^ 1, x, zl))
-    here = jnp.stack([dot_t(ours, block) for block in blocks])
-    chip = (here + other.astype(jnp.float32)).astype(jnp.bfloat16)
+    chip = partial_product(ours, blocks, other)
 
-    chip, mine = lax.optimization_barrier((chip, mine))
     shares = lax.all_to_all(chip, AXES, 0, 0, axis_index_groups=swap_groups())
     beside = send(mine, lambda zh, y, core, x, zl: (zh, y, core ^ 1, x, zl))
     across = jnp.concatenate([jnp.where(core == 0, mine, beside), jnp.where(core == 0, beside, mine)])

time: 185 us -> 179 us (0.968); the launches traced: 184 us -> 176 us
  starting transfers between devices: 90 us -> 82.6 us
  waiting for transfers between devices: 72.7 us -> 80.1 us
  matrix products: 6.01 us -> 0.87 us
  other arithmetic: 9.75 us -> 4.69 us
  Pallas kernels: 0 us -> 3.53 us
    all_to_all x1, starting transfers between devices: 15.9 us -> 5.42 us  [per_device(): pieces = lax.all_to_all(terms.reshape(32, 8, 128), 'pcol', 0, 0)]
    ppermute x13, waiting for transfers between devices: 39.2 us -> 46.6 us  [send(): return lax.ppermute(value, AXES, pairs)]
    dot_general x9 -> x1, matrix products: 6.01 us -> 0.87 us  [dot_t(): lax.dot_general(left, right, CONTRACT_LAST, preferred_element_type=jnp.fl...]
    pallas_call x0 -> x2, Pallas kernels: none -> 3.53 us  [partial_product(): pl.pallas_call(functools.partial(product_kernel, len(added)), in_specs=[p...]
    ppermute x13, starting transfers between devices: 65.7 us -> 68.8 us  [send(): return lax.ppermute(value, AXES, pairs)]
    convert_element_type x1 -> x0, other arithmetic: 2.61 us -> none  [per_device(): chip = (here + other.astype(jnp.float32)).astype(jnp.bfloat16)]
  transfers between devices with their start and end apart: 16 -> 16, of which waited for: 9 -> 10; matrix products, arithmetic and copies ran while one was open for 7% -> 3% of each run, Pallas kernels for 0% -> 1%
where the time goes in v3:
time: 179 us; the launch traced here: 176 us
  starting transfers between devices  82.6 us (46%)
  waiting for transfers between devices  80.1 us (45%)
  other arithmetic  4.69 us (3%)
  Pallas kernels  3.53 us (2%)
  local copies, waits for them, and re-layouts  3.13 us (2%)
    ppermute x13, starting transfers between devices, send(): return lax.ppermute(value, AXES, pairs)  68.8 us
    ppermute x13, waiting for transfers between devices, send(): return lax.ppermute(value, AXES, pairs)  46.6 us
    all_to_all x1, waiting for transfers between devices, per_device(): pieces = lax.all_to_all(terms.reshape(32, 8, 128), 'pcol', 0, 0)  11.8 us
    all_to_all x1, waiting for transfers between devices, per_device(): lax.all_to_all(jnp.broadcast_to(piece[None], (32, 8, 128)), 'pcol', 0, 0)  11.1 us
    all_to_all x1, waiting for transfers between devices, per_device(): shares = lax.all_to_all(chip, AXES, 0, 0, axis_index_groups=swap_groups())  10.7 us
    all_to_all x1, starting transfers between devices, per_device(): pieces = lax.all_to_all(terms.reshape(32, 8, 128), 'pcol', 0, 0)  5.42 us
    all_to_all x1, starting transfers between devices, per_device(): shares = lax.all_to_all(chip, AXES, 0, 0, axis_index_groups=swap_groups())  4.5 us
    all_to_all x1, starting transfers between devices, per_device(): lax.all_to_all(jnp.broadcast_to(piece[None], (32, 8, 128)), 'pcol', 0, 0)  3.92 us
  transfers between devices with their start and end apart: 16, of which 10 were waited for; matrix products, arithmetic and copies ran while one was open for 3% of the time, Pallas kernels for 1%

profile of v3, /device:TPU:24, one launch (start us, length us, event | category | flops | bytes accessed | tf_op | source)
XLA Modules:
  0.0 175.9 jit_solution(6832291442438046245)
XLA Ops:
  0.6 9.1 %collective-permute-start.1 = (bf16[64,1024]{1,0:T(8,128)(2,1)}, bf16[64,1024]{1,0:T(8,128)(2,1)S(1)}, u32[]{:S(2)}, u32[]{:S(2)}) collective-permute-start(bf16[64,1024]{1,0:T(8,128)(2,1)} %bitcast.37), channel_id=1, source_target_pairs={{0,4},{1,5},{2,6},{3,7},{4,12},{5,13},{6,14},{7,15},{8,20},{9,21},... | collective-permute-start | bytes 393224 | tf_op jit(solution)/shard_map/ppermute | solution.py:22
  9.7 1.6 collective-permute-start
  11.3 4.7 %collective-permute-start.6 = (bf16[512,1024]{1,0:T(8,128)(2,1)}, bf16[512,1024]{1,0:T(8,128)(2,1)S(1)}, u32[]{:S(2)}, u32[]{:S(2)}) collective-permute-start(bf16[512,1024]{1,0:T(8,128)(2,1)} %near.3), channel_id=1, source_target_pairs={{0,8},{1,9},{2,10},{3,11},{4,12},{5,13},{6,14},{7,15},{8,0},{9,1},... | collective-permute-start | bytes 3145736 | tf_op jit(solution)/shard_map/ppermute | solution.py:22
  16.0 4.5 %collective-permute-start.4 = (bf16[512,1024]{1,0:T(8,128)(2,1)}, bf16[512,1024]{1,0:T(8,128)(2,1)S(1)}, u32[]{:S(2)}, u32[]{:S(2)}) collective-permute-start(bf16[512,1024]{1,0:T(8,128)(2,1)} %near.3), channel_id=1, source_target_pairs={{0,24},{1,25},{2,26},{3,27},{4,28},{5,29},{6,30},{7,31},{8,16},{9,... | collective-permute-start | bytes 3145736 | tf_op jit(solution)/shard_map/ppermute | solution.py:22
  21.9 5.2 %collective-permute-start.2 = (bf16[2,64,1024]{2,1,0:T(8,128)(2,1)S(1)}, bf16[2,64,1024]{2,1,0:T(8,128)(2,1)S(1)}, u32[]{:S(2)}, u32[]{:S(2)}) collective-permute-start(bf16[2,64,1024]{2,1,0:T(8,128)(2,1)S(1)} %get-tuple-element.27), channel_id=1, source_target_pairs={{0,2},{1,3},{2,0},{3,1},{4,6},{5,7},{6,4},{7,5},{8,10},{9,11},{10,... | collective-permute-start | bytes 786440 | tf_op jit(solution)/shard_map/ppermute | solution.py:22
  28.0 12.6 %collective-permute-done.2 = bf16[2,64,1024]{2,1,0:T(8,128)(2,1)S(1)} collective-permute-done((bf16[2,64,1024]{2,1,0:T(8,128)(2,1)S(1)}, bf16[2,64,1024]{2,1,0:T(8,128)(2,1)S(1)}, u32[]{:S(2)}, u32[]{:S(2)}) %collective-permute-start.2) | collective-permute-done | bytes 262176 | tf_op jit(solution)/shard_map/ppermute | solution.py:22
  40.6 1.9 %collective-permute-start.3 = (bf16[2,2,64,1024]{3,2,0,1:T(8,128)(2,1)S(1)}, bf16[2,2,64,1024]{3,2,0,1:T(8,128)(2,1)S(1)}, u32[]{:S(2)}, u32[]{:S(2)}) collective-permute-start(bf16[2,2,64,1024]{3,2,0,1:T(8,128)(2,1)S(1)} %pad_maximum_fusion), channel_id=1, source_target_pairs={{0,1},{1,0},{2,3},{3,2},{4,5},{5,4},{6,7},{7,6},{8,9},{9,8},{10,11... | collective-permute-start | bytes 1572872 | tf_op jit(solution)/shard_map/ppermute | solution.py:22
  42.8 4.8 %collective-permute-start.7 = (bf16[256,1024]{1,0:T(8,128)(2,1)S(1)}, bf16[256,1024]{1,0:T(8,128)(2,1)S(1)}, u32[]{:S(2)}, u32[]{:S(2)}) collective-permute-start(bf16[256,1024]{1,0:T(8,128)(2,1)S(1)} %slice.13), channel_id=1, source_target_pairs={{0,24},{1,25},{2,26},{3,27},{4,28},{5,29},{6,30},{7,31},{8,16},{9,... | collective-permute-start | bytes 1572872 | tf_op jit(solution)/shard_map/ppermute | solution.py:22
  47.6 2.0 %collective-permute-start.5 = (bf16[256,1024]{1,0:T(8,128)(2,1)S(1)}, bf16[256,1024]{1,0:T(8,128)(2,1)S(1)}, u32[]{:S(2)}, u32[]{:S(2)}) collective-permute-start(bf16[256,1024]{1,0:T(8,128)(2,1)S(1)} %slice.12), channel_id=1, source_target_pairs={{0,8},{1,9},{2,10},{3,11},{4,12},{5,13},{6,14},{7,15},{8,0},{9,1},... | collective-permute-start | bytes 1572872 | tf_op jit(solution)/shard_map/ppermute | solution.py:22
  49.6 5.0 %collective-permute-done.3 = bf16[2,2,64,1024]{3,2,0,1:T(8,128)(2,1)S(1)} collective-permute-done((bf16[2,2,64,1024]{3,2,0,1:T(8,128)(2,1)S(1)}, bf16[2,2,64,1024]{3,2,0,1:T(8,128)(2,1)S(1)}, u32[]{:S(2)}, u32[]{:S(2)}) %collective-permute-start.3) | collective-permute-done | bytes 524320 | tf_op jit(solution)/shard_map/ppermute | solution.py:22
  54.9 4.1 %collective-permute-start.8 = (bf16[128,512]{1,0:T(8,128)(2,1)S(1)}, bf16[128,512]{1,0:T(8,128)(2,1)S(1)}, u32[]{:S(2)}, u32[]{:S(2)}) collective-permute-start(bf16[128,512]{1,0:T(8,128)(2,1)S(1)} %constant_dynamic-slice_fusion), channel_id=1, source_target_pairs={{0,0},{1,1},{2,32},{3,33},{4,256},{5,257},{6,288},{7,289},{8,64},{... | collective-permute-start | bytes 393224 | tf_op jit(solution)/shard_map/ppermute | solution.py:22
  59.7 3.4 %collective-permute-done.5.upper = bf16[256,1024]{1,0:T(8,128)(2,1)S(1)} collective-permute-done((bf16[256,1024]{1,0:T(8,128)(2,1)S(1)}, bf16[256,1024]{1,0:T(8,128)(2,1)S(1)}, u32[]{:S(2)}, u32[]{:S(2)}) %collective-permute-start.5) | collective-permute-done | bytes 524320 | tf_op jit(solution)/shard_map/ppermute | solution.py:22
  63.1 1.3 shard_map.77
  64.4 4.4 %collective-permute-done.8 = bf16[128,512]{1,0:T(8,128)(2,1)S(1)} collective-permute-done((bf16[128,512]{1,0:T(8,128)(2,1)S(1)}, bf16[128,512]{1,0:T(8,128)(2,1)S(1)}, u32[]{:S(2)}, u32[]{:S(2)}) %collective-permute-start.8) | collective-permute-done | bytes 131104 | tf_op jit(solution)/shard_map/ppermute | solution.py:22
  68.8 1.9 %collective-permute-start.9 = (bf16[4,256,512]{2,1,0:T(8,128)(2,1)S(1)}, bf16[4,256,512]{2,1,0:T(8,128)(2,1)S(1)}, u32[]{:S(2)}, u32[]{:S(2)}) collective-permute-start(bf16[4,256,512]{2,1,0:T(8,128)(2,1)S(1)} %shard_map.77), channel_id=1, source_target_pairs={{0,32},{1,33},{2,34},{3,35},{4,36},{5,37},{6,38},{7,39},{8,40},{9,... | collective-permute-start | bytes 3145736 | tf_op jit(solution)/shard_map/ppermute | solution.py:22
  70.7 2.6 %collective-permute-done.9.rest_0_ = bf16[4,256,512]{2,1,0:T(8,128)(2,1)S(1)} collective-permute-done((bf16[4,256,512]{2,1,0:T(8,128)(2,1)S(1)}, bf16[4,256,512]{2,1,0:T(8,128)(2,1)S(1)}, u32[]{:S(2)}, u32[]{:S(2)}) %collective-permute-start.9) | collective-permute-done | bytes 1048608 | tf_op jit(solution)/shard_map/ppermute | solution.py:22
  73.4 2.3 %shard_map.78 = bf16[4,256,512]{2,1,0:T(8,128)(2,1)} custom-call(bf16[256,1024]{1,0:T(8,128)(2,1)S(1)} %bitcast.28, bf16[512,1024]{1,0:T(8,128)(2,1)S(1)} %copy-done, bf16[512,1024]{1,0:T(8,128)(2,1)S(1)} %collective-permute-done.6.one, bf16[256,1024]{1,0:T(8,128)(2,1)S(1)} %collective-permute-done.5.upper, ...), custom_call_target="tpu_custom_call" | custom-call | flops 1073741824 | bytes 5767168 | tf_op jit(solution)/shard_map/pallas_call | solution.py:68
  75.6 4.5 %all-to-all-start = ((bf16[4,256,512]{2,1,0:T(8,128)(2,1)}), bf16[4,256,512]{2,1,0:T(8,128)(2,1)S(1)}, u32[]{:S(2)}, u32[]{:S(2)}) async-start(bf16[4,256,512]{2,1,0:T(8,128)(2,1)} %shard_map.78), calls=%async_computation | async-start | bytes 2097152 | tf_op jit(solution)/shard_map/all_to_all | solution.py:138
  80.2 1.9 %collective-permute-start.12 = (bf16[128,512]{1,0:T(8,128)(2,1)S(1)}, bf16[128,512]{1,0:T(8,128)(2,1)S(1)}, u32[]{:S(2)}, u32[]{:S(2)}) collective-permute-start(bf16[128,512]{1,0:T(8,128)(2,1)S(1)} %collective-permute-done.8), channel_id=1, source_target_pairs={{0,32},{1,33},{2,34},{3,35},{4,36},{5,37},{6,38},{7,39},{8,40},{9,... | collective-permute-start | bytes 393224 | tf_op jit(solution)/shard_map/ppermute | solution.py:22
  82.8 10.7 %all-to-all-done = bf16[4,256,512]{2,1,0:T(8,128)(2,1)S(1)} async-done(((bf16[4,256,512]{2,1,0:T(8,128)(2,1)}), bf16[4,256,512]{2,1,0:T(8,128)(2,1)S(1)}, u32[]{:S(2)}, u32[]{:S(2)}) %all-to-all-start) | async-done | bytes 1048608 | tf_op jit(solution)/shard_map/all_to_all | solution.py:138
  93.7 18.5 %collective-permute-start.10 = (bf16[128,512]{1,0:T(8,128)(2,1)S(1)}, bf16[128,512]{1,0:T(8,128)(2,1)S(1)}, u32[]{:S(2)}, u32[]{:S(2)}) collective-permute-start(bf16[128,512]{1,0:T(8,128)(2,1)S(1)} %get-tuple-element.24), channel_id=1, source_target_pairs={{0,0},{1,1},{2,2},{3,3},{4,4},{5,5},{6,6},{7,7},{8,64},{9,65},{10,... | collective-permute-start | bytes 393224 | tf_op jit(solution)/shard_map/ppermute | solution.py:22
  112.2 8.7 %collective-permute-start.11 = (bf16[128,512]{1,0:T(8,128)(2,1)S(1)}, bf16[128,512]{1,0:T(8,128)(2,1)S(1)}, u32[]{:S(2)}, u32[]{:S(2)}) collective-permute-start(bf16[128,512]{1,0:T(8,128)(2,1)S(1)} %get-tuple-element.25), channel_id=1, source_target_pairs={{0,256},{1,257},{2,258},{3,259},{4,260},{5,261},{6,262},{7,263},{8... | collective-permute-start | bytes 393224 | tf_op jit(solution)/shard_map/ppermute | solution.py:22
  120.9 18.0 %collective-permute-done.11 = bf16[128,512]{1,0:T(8,128)(2,1)S(1)} collective-permute-done((bf16[128,512]{1,0:T(8,128)(2,1)S(1)}, bf16[128,512]{1,0:T(8,128)(2,1)S(1)}, u32[]{:S(2)}, u32[]{:S(2)}) %collective-permute-start.11) | collective-permute-done | bytes 131104 | tf_op jit(solution)/shard_map/ppermute | solution.py:22
  138.9 0.9 fusion
  139.8 5.4 %all-to-all-start.1 = ((bf16[32,8,128]{2,1,0:T(8,128)(2,1)}), bf16[32,8,128]{2,1,0:T(8,128)(2,1)S(1)}, u32[]{:S(2)}, u32[]{:S(2)}) async-start(bf16[32,8,128]{2,1,0:T(8,128)(2,1)} %fusion), calls=%async_computation.1 | async-start | bytes 131072 | tf_op jit(solution)/shard_map/all_to_all | solution.py:150
  145.3 0.7 iota_compare_fusion.3
  146.1 11.8 %all-to-all-done.1 = bf16[32,8,128]{2,1,0:T(8,128)(2,1)S(1)} async-done(((bf16[32,8,128]{2,1,0:T(8,128)(2,1)}), bf16[32,8,128]{2,1,0:T(8,128)(2,1)S(1)}, u32[]{:S(2)}, u32[]{:S(2)}) %all-to-all-start.1) | async-done | bytes 65568 | tf_op jit(solution)/shard_map/all_to_all | solution.py:150
  158.6 3.9 %all-to-all-start.2 = ((bf16[32,8,128]{2,1,0:T(8,128)(2,1)}), bf16[32,8,128]{2,1,0:T(8,128)(2,1)S(1)}, u32[]{:S(2)}, u32[]{:S(2)}) async-start(bf16[32,8,128]{2,1,0:T(8,128)(2,1)} %broadcast_in_dim.83), calls=%async_computation.2 | async-start | bytes 131072 | tf_op jit(solution)/shard_map/all_to_all | solution.py:152
  162.5 0.7 add_compare_fusion
  163.3 0.8 copy.17
  164.1 11.1 %all-to-all-done.2 = bf16[32,8,128]{2,1,0:T(8,128)(2,1)S(1)} async-done(((bf16[32,8,128]{2,1,0:T(8,128)(2,1)}), bf16[32,8,128]{2,1,0:T(8,128)(2,1)S(1)}, u32[]{:S(2)}, u32[]{:S(2)}) %all-to-all-start.2) | async-done | bytes 65568 | tf_op jit(solution)/shard_map/all_to_all | solution.py:152
  175.1 0.8 convert_add_fusion.1
  (56 shorter events, 5.4 us)
Async XLA Ops:
  0.6 21.2 %collective-permute-start.1 = (bf16[64,1024]{1,0:T(8,128)(2,1)}, bf16[64,1024]{1,0:T(8,128)(2,1)S(1)}, u32[]{:S(2)}, u32[]{:S(2)}) collective-permute-start(bf16[64,1024]{1,0:T(8,128)(2,1)} %bitcast.37), channel_id=1, source_target_pairs={{0,4},{1,5},{2,6},{3,7},{4,12},{5,13},{6,14},{7,15},{8,20},{9,21},... | collective-permute-start | bytes 393224 | tf_op jit(solution)/shard_map/ppermute | solution.py:22
  9.7 12.1 %collective-permute-start = (bf16[64,1024]{1,0:T(8,128)(2,1)}, bf16[64,1024]{1,0:T(8,128)(2,1)S(1)}, u32[]{:S(2)}, u32[]{:S(2)}) collective-permute-start(bf16[64,1024]{1,0:T(8,128)(2,1)} %bitcast.38), channel_id=1, source_target_pairs={{0,0},{1,1},{2,2},{3,3},{4,8},{5,9},{6,10},{7,11},{8,16},{9,17},{1... | collective-permute-start | bytes 393224 | tf_op jit(solution)/shard_map/ppermute | solution.py:22
  11.3 31.4 %collective-permute-start.6 = (bf16[512,1024]{1,0:T(8,128)(2,1)}, bf16[512,1024]{1,0:T(8,128)(2,1)S(1)}, u32[]{:S(2)}, u32[]{:S(2)}) collective-permute-start(bf16[512,1024]{1,0:T(8,128)(2,1)} %near.3), channel_id=1, source_target_pairs={{0,8},{1,9},{2,10},{3,11},{4,12},{5,13},{6,14},{7,15},{8,0},{9,1},... | collective-permute-start | bytes 3145736 | tf_op jit(solution)/shard_map/ppermute | solution.py:22
  16.0 31.6 %collective-permute-start.4 = (bf16[512,1024]{1,0:T(8,128)(2,1)}, bf16[512,1024]{1,0:T(8,128)(2,1)S(1)}, u32[]{:S(2)}, u32[]{:S(2)}) collective-permute-start(bf16[512,1024]{1,0:T(8,128)(2,1)} %near.3), channel_id=1, source_target_pairs={{0,24},{1,25},{2,26},{3,27},{4,28},{5,29},{6,30},{7,31},{8,16},{9,... | collective-permute-start | bytes 3145736 | tf_op jit(solution)/shard_map/ppermute | solution.py:22
  20.5 0.7 copy-start.2
  20.6 0.7 copy-start.3
  21.9 18.7 %collective-permute-start.2 = (bf16[2,64,1024]{2,1,0:T(8,128)(2,1)S(1)}, bf16[2,64,1024]{2,1,0:T(8,128)(2,1)S(1)}, u32[]{:S(2)}, u32[]{:S(2)}) collective-permute-start(bf16[2,64,1024]{2,1,0:T(8,128)(2,1)S(1)} %get-tuple-element.27), channel_id=1, source_target_pairs={{0,2},{1,3},{2,0},{3,1},{4,6},{5,7},{6,4},{7,5},{8,10},{9,11},{10,... | collective-permute-start | bytes 786440 | tf_op jit(solution)/shard_map/ppermute | solution.py:22
  27.1 0.7 copy-start.4
  40.6 14.0 %collective-permute-start.3 = (bf16[2,2,64,1024]{3,2,0,1:T(8,128)(2,1)S(1)}, bf16[2,2,64,1024]{3,2,0,1:T(8,128)(2,1)S(1)}, u32[]{:S(2)}, u32[]{:S(2)}) collective-permute-start(bf16[2,2,64,1024]{3,2,0,1:T(8,128)(2,1)S(1)} %pad_maximum_fusion), channel_id=1, source_target_pairs={{0,1},{1,0},{2,3},{3,2},{4,5},{5,4},{6,7},{7,6},{8,9},{9,8},{10,11... | collective-permute-start | bytes 1572872 | tf_op jit(solution)/shard_map/ppermute | solution.py:22
  42.8 16.9 %collective-permute-start.7 = (bf16[256,1024]{1,0:T(8,128)(2,1)S(1)}, bf16[256,1024]{1,0:T(8,128)(2,1)S(1)}, u32[]{:S(2)}, u32[]{:S(2)}) collective-permute-start(bf16[256,1024]{1,0:T(8,128)(2,1)S(1)} %slice.13), channel_id=1, source_target_pairs={{0,24},{1,25},{2,26},{3,27},{4,28},{5,29},{6,30},{7,31},{8,16},{9,... | collective-permute-start | bytes 1572872 | tf_op jit(solution)/shard_map/ppermute | solution.py:22
  47.6 15.5 %collective-permute-start.5 = (bf16[256,1024]{1,0:T(8,128)(2,1)S(1)}, bf16[256,1024]{1,0:T(8,128)(2,1)S(1)}, u32[]{:S(2)}, u32[]{:S(2)}) collective-permute-start(bf16[256,1024]{1,0:T(8,128)(2,1)S(1)} %slice.12), channel_id=1, source_target_pairs={{0,8},{1,9},{2,10},{3,11},{4,12},{5,13},{6,14},{7,15},{8,0},{9,1},... | collective-permute-start | bytes 1572872 | tf_op jit(solution)/shard_map/ppermute | solution.py:22
  54.9 13.9 %collective-permute-start.8 = (bf16[128,512]{1,0:T(8,128)(2,1)S(1)}, bf16[128,512]{1,0:T(8,128)(2,1)S(1)}, u32[]{:S(2)}, u32[]{:S(2)}) collective-permute-start(bf16[128,512]{1,0:T(8,128)(2,1)S(1)} %constant_dynamic-slice_fusion), channel_id=1, source_target_pairs={{0,0},{1,1},{2,32},{3,33},{4,256},{5,257},{6,288},{7,289},{8,64},{... | collective-permute-start | bytes 393224 | tf_op jit(solution)/shard_map/ppermute | solution.py:22
  59.1 4.0 %copy-start = (bf16[512,1024]{1,0:T(8,128)(2,1)S(1)}, bf16[512,1024]{1,0:T(8,128)(2,1)}, u32[]{:S(2)}) copy-start(bf16[512,1024]{1,0:T(8,128)(2,1)} %near.3) | copy-start | bytes 3145732
  68.8 4.5 %collective-permute-start.9 = (bf16[4,256,512]{2,1,0:T(8,128)(2,1)S(1)}, bf16[4,256,512]{2,1,0:T(8,128)(2,1)S(1)}, u32[]{:S(2)}, u32[]{:S(2)}) collective-permute-start(bf16[4,256,512]{2,1,0:T(8,128)(2,1)S(1)} %shard_map.77), channel_id=1, source_target_pairs={{0,32},{1,33},{2,34},{3,35},{4,36},{5,37},{6,38},{7,39},{8,40},{9,... | collective-permute-start | bytes 3145736 | tf_op jit(solution)/shard_map/ppermute | solution.py:22
  75.6 17.8 %all-to-all-start = ((bf16[4,256,512]{2,1,0:T(8,128)(2,1)}), bf16[4,256,512]{2,1,0:T(8,128)(2,1)S(1)}, u32[]{:S(2)}, u32[]{:S(2)}) async-start(bf16[4,256,512]{2,1,0:T(8,128)(2,1)} %shard_map.78), calls=%async_computation | async-start | bytes 2097152 | tf_op jit(solution)/shard_map/all_to_all | solution.py:138
  80.2 40.7 %collective-permute-start.12 = (bf16[128,512]{1,0:T(8,128)(2,1)S(1)}, bf16[128,512]{1,0:T(8,128)(2,1)S(1)}, u32[]{:S(2)}, u32[]{:S(2)}) collective-permute-start(bf16[128,512]{1,0:T(8,128)(2,1)S(1)} %collective-permute-done.8), channel_id=1, source_target_pairs={{0,32},{1,33},{2,34},{3,35},{4,36},{5,37},{6,38},{7,39},{8,40},{9,... | collective-permute-start | bytes 393224 | tf_op jit(solution)/shard_map/ppermute | solution.py:22
  93.7 27.2 %collective-permute-start.10 = (bf16[128,512]{1,0:T(8,128)(2,1)S(1)}, bf16[128,512]{1,0:T(8,128)(2,1)S(1)}, u32[]{:S(2)}, u32[]{:S(2)}) collective-permute-start(bf16[128,512]{1,0:T(8,128)(2,1)S(1)} %get-tuple-element.24), channel_id=1, source_target_pairs={{0,0},{1,1},{2,2},{3,3},{4,4},{5,5},{6,6},{7,7},{8,64},{9,65},{10,... | collective-permute-start | bytes 393224 | tf_op jit(solution)/shard_map/ppermute | solution.py:22
  112.2 26.7 %collective-permute-start.11 = (bf16[128,512]{1,0:T(8,128)(2,1)S(1)}, bf16[128,512]{1,0:T(8,128)(2,1)S(1)}, u32[]{:S(2)}, u32[]{:S(2)}) collective-permute-start(bf16[128,512]{1,0:T(8,128)(2,1)S(1)} %get-tuple-element.25), channel_id=1, source_target_pairs={{0,256},{1,257},{2,258},{3,259},{4,260},{5,261},{6,262},{7,263},{8... | collective-permute-start | bytes 393224 | tf_op jit(solution)/shard_map/ppermute | solution.py:22
  139.8 18.1 %all-to-all-start.1 = ((bf16[32,8,128]{2,1,0:T(8,128)(2,1)}), bf16[32,8,128]{2,1,0:T(8,128)(2,1)S(1)}, u32[]{:S(2)}, u32[]{:S(2)}) async-start(bf16[32,8,128]{2,1,0:T(8,128)(2,1)} %fusion), calls=%async_computation.1 | async-start | bytes 131072 | tf_op jit(solution)/shard_map/all_to_all | solution.py:150
  158.6 16.6 %all-to-all-start.2 = ((bf16[32,8,128]{2,1,0:T(8,128)(2,1)}), bf16[32,8,128]{2,1,0:T(8,128)(2,1)S(1)}, u32[]{:S(2)}, u32[]{:S(2)}) async-start(bf16[32,8,128]{2,1,0:T(8,128)(2,1)} %broadcast_in_dim.83), calls=%async_computation.2 | async-start | bytes 131072 | tf_op jit(solution)/shard_map/all_to_all | solution.py:152
  163.3 11.8 %copy-start.1 = (f32[256,128]{1,0:T(8,128)S(1)}, f32[256,128]{1,0:T(8,128)}, u32[]{:S(2)}) copy-start(f32[256,128]{1,0:T(8,128)} %param.8) | copy-start | bytes 393220

commit v4 on v3

--- a/solution.py
+++ b/solution.py
@@ -27,8 +27,9 @@
     return (zh, y, core, node & 3, (((node >> 2) ^ flip) << 2) | (zl & 3))
 
 
-def rows_home(zh, y, core, x, zl):
-    return (zl >> 2, x, (zl >> 1) & 1, (zh << 1) | (y >> 1), ((y & 1) << 2) | (core << 1) | (zl & 1))
+def rows_home(zh, y, core, x, zl, flip):
+    column = ((y & 1) << 2) | (core << 1) | ((zl & 1) ^ flip)
+    return (x >> 1, ((x & 1) << 1) | (zl >> 2), (zl >> 1) & 1, (zh << 1) | (y >> 1), column)
 
 
 def swap_groups():
@@ -88,13 +89,22 @@
     own = lpanel.T
     first = send(own, lambda *d: fold_x(*d, 0))
     second = send(own, lambda *d: fold_x(*d, 1))
+    panel, first, second = lax.optimization_barrier((own, first, second))
     pair = jnp.stack([first, second])
+    mine = [
+        send(
+            lax.dynamic_slice_in_dim(panel, (low ^ k) * 512, 512, axis=1),
+            lambda *d: rows_home(*d, k),
+        )
+        for k in range(2)
+    ]
     near = send(pair, lambda zh, y, core, x, zl: (zh, y, core, x, zl ^ 2))
+    a1 = send(ainv, lambda zh, y, core, x, zl: (zh, y, core, x ^ 1, zl))
+    a3 = send(ainv, lambda zh, y, core, x, zl: (zh, y, core, x ^ 3, zl))
     quad = jnp.stack([pair, near], axis=1)
+    quad, a1, a3 = lax.optimization_barrier((quad, a1, a3))
     last = send(quad, lambda zh, y, core, x, zl: (zh, y, core, x, zl ^ 1))
 
-    a1 = send(ainv, lambda zh, y, core, x, zl: (zh, y, core, x ^ 1, zl))
-    a3 = send(ainv, lambda zh, y, core, x, zl: (zh, y, core, x ^ 3, zl))
     half = ainv.shape[0] // 2
     a2 = [
         send(a3[:half], lambda zh, y, core, x, zl: (zh, y, core, x ^ 1, zl)),
@@ -117,14 +127,25 @@
     within = half_of + jnp.arange(128, dtype=jnp.int32).reshape(1, 2, 64)
     active = within[None] < width[:, None, None, None]
 
+    node = prow >> 1
+    row_ids = pcol * 2 + jnp.arange(2, dtype=jnp.int32)
+    kept = jnp.any(
+        (row_ids[:, None] == jnp.arange(64, dtype=jnp.int32)[None, :])[:, None, :]
+        & (nodes == node)[None, :, None]
+        & member[None],
+        axis=(1, 2),
+    )
+    my_width = jnp.sum(jnp.where(nodes == node, widths, 0))
+    column = core * 128 + jnp.arange(128, dtype=jnp.int32)
+    mine = jnp.concatenate([jnp.where(low == 0, mine[0], mine[1]), jnp.where(low == 0, mine[1], mine[0])])
+    mine = mine * (column < my_width).astype(jnp.bfloat16)[:, None]
+    mine = mine * jnp.repeat(kept.astype(jnp.bfloat16), B)[None, :]
+
     factor = jnp.stack(
         [jnp.where(low == 0, quad, last), jnp.where(low == 0, last, quad)], axis=2
     )
     row_scale = jnp.repeat(live.astype(jnp.bfloat16), B, axis=1)
     factor = factor * active[..., None].astype(jnp.bfloat16) * row_scale[:, None, None, None, :]
-
-    mine = lax.dynamic_slice_in_dim(factor[0, 0].reshape(128, 1024), low * 512, 512, axis=1)
-    mine = send(mine, rows_home)
 
     keep = core ^ mid
     theirs = lax.dynamic_index_in_dim(factor, 1 - keep, 1, keepdims=False).reshape(256, 1024)
@@ -152,19 +173,9 @@
     terms = lax.all_to_all(jnp.broadcast_to(piece[None], (32, 8, 128)), "pcol", 0, 0)
     terms = terms.reshape(256, 128).astype(jnp.float32)
 
-    node = prow >> 1
-    row_ids = pcol * 2 + jnp.arange(2, dtype=jnp.int32)
-    kept = jnp.any(
-        (row_ids[:, None] == jnp.arange(64, dtype=jnp.int32)[None, :])[:, None, :]
-        & (nodes == node)[None, :, None]
-        & member[None],
-        axis=(1, 2),
-    )
     negated = jnp.where(kept[None, :, None], -product.reshape(128, 2, B), 0.0).reshape(128, 512)
     selected_inverse = negated.astype(jnp.bfloat16).T
 
-    my_width = jnp.sum(jnp.where(nodes == node, widths, 0))
-    column = core * 128 + jnp.arange(128, dtype=jnp.int32)
     corner = (jnp.arange(B, dtype=jnp.int32)[:, None] < my_width) & (column < my_width)[None, :]
     diagonal_blocks = jnp.where(corner, dinv, 0.0) + terms
     return (selected_inverse, diagonal_blocks)

time: 179 us -> 175 us (0.978); the launches traced: 176 us -> 174 us
  waiting for transfers between devices: 80.1 us -> 53.7 us
  blocking collectives: 0 us -> 23.2 us
    all_to_all x0 -> x1, blocking collectives: none -> 23.2 us  [per_device(): pieces = lax.all_to_all(terms.reshape(32, 8, 128), 'pcol', 0, 0)]
    ppermute x13 -> x14, waiting for transfers between devices: 46.6 us -> 31.3 us  [send(): return lax.ppermute(value, AXES, pairs)]
    all_to_all x1 -> x0, waiting for transfers between devices: 11.8 us -> none  [per_device(): pieces = lax.all_to_all(terms.reshape(32, 8, 128), 'pcol', 0, 0)]
    all_to_all x1, starting transfers between devices: 4.5 us -> 10.4 us  [per_device(): shares = lax.all_to_all(chip, AXES, 0, 0, axis_index_groups=swap_groups())]
    all_to_all x1 -> x0, starting transfers between devices: 5.42 us -> none  [per_device(): pieces = lax.all_to_all(terms.reshape(32, 8, 128), 'pcol', 0, 0)]
    ppermute x13 -> x14, starting transfers between devices: 68.8 us -> 70 us  [send(): return lax.ppermute(value, AXES, pairs)]
  transfers between devices with their start and end apart: 16 -> 16, of which waited for: 10 -> 9; matrix products, arithmetic and copies ran while one was open for 3% -> 3% of each run, Pallas kernels for 1% -> 0%
where the time goes in v4:
time: 175 us; the launch traced here: 174 us
  starting transfers between devices  84.3 us (48%)
  waiting for transfers between devices  53.7 us (31%)
  blocking collectives  23.2 us (13%)
  other arithmetic  4.8 us (3%)
  Pallas kernels  3.54 us (2%)
  local copies, waits for them, and re-layouts  3.24 us (2%)
    ppermute x14, starting transfers between devices, send(): return lax.ppermute(value, AXES, pairs)  70 us
    ppermute x14, waiting for transfers between devices, send(): return lax.ppermute(value, AXES, pairs)  31.3 us
    all_to_all x1, blocking collectives, per_device(): pieces = lax.all_to_all(terms.reshape(32, 8, 128), 'pcol', 0, 0)  23.2 us
    all_to_all x1, waiting for transfers between devices, per_device(): shares = lax.all_to_all(chip, AXES, 0, 0, axis_index_groups=swap_groups())  11.4 us
    all_to_all x1, waiting for transfers between devices, per_device(): lax.all_to_all(jnp.broadcast_to(piece[None], (32, 8, 128)), 'pcol', 0, 0)  11.1 us
    all_to_all x1, starting transfers between devices, per_device(): shares = lax.all_to_all(chip, AXES, 0, 0, axis_index_groups=swap_groups())  10.4 us
    all_to_all x1, starting transfers between devices, per_device(): lax.all_to_all(jnp.broadcast_to(piece[None], (32, 8, 128)), 'pcol', 0, 0)  3.92 us
    pallas_call x2, Pallas kernels, partial_product(): pl.pallas_call(functools.partial(product_kernel, len(added)), in_specs=[p...  3.54 us
  transfers between devices with their start and end apart: 16, of which 9 were waited for; matrix products, arithmetic and copies ran while one was open for 3% of the time, Pallas kernels for 0%

profile of v4, /device:TPU:24, one launch (start us, length us, event | category | flops | bytes accessed | tf_op | source)
XLA Modules:
  0.0 174.2 jit_solution(2158481634635390509)
XLA Ops:
  0.6 1.6 collective-permute-start
  2.2 9.5 %collective-permute-start.1 = (bf16[64,1024]{1,0:T(8,128)(2,1)}, bf16[64,1024]{1,0:T(8,128)(2,1)S(1)}, u32[]{:S(2)}, u32[]{:S(2)}) collective-permute-start(bf16[64,1024]{1,0:T(8,128)(2,1)} %bitcast.35), channel_id=1, source_target_pairs={{0,4},{1,5},{2,6},{3,7},{4,12},{5,13},{6,14},{7,15},{8,20},{9,21},... | collective-permute-start | bytes 393224 | tf_op jit(solution)/shard_map/ppermute | solution.py:22
  11.7 4.9 %collective-permute-start.3 = (bf16[512,1024]{1,0:T(8,128)(2,1)}, bf16[512,1024]{1,0:T(8,128)(2,1)S(1)}, u32[]{:S(2)}, u32[]{:S(2)}) collective-permute-start(bf16[512,1024]{1,0:T(8,128)(2,1)} %near.3), channel_id=1, source_target_pairs={{0,8},{1,9},{2,10},{3,11},{4,12},{5,13},{6,14},{7,15},{8,0},{9,1},... | collective-permute-start | bytes 3145736 | tf_op jit(solution)/shard_map/ppermute | solution.py:22
  16.5 2.5 %collective-permute-start.4 = (bf16[512,1024]{1,0:T(8,128)(2,1)}, bf16[512,1024]{1,0:T(8,128)(2,1)S(1)}, u32[]{:S(2)}, u32[]{:S(2)}) collective-permute-start(bf16[512,1024]{1,0:T(8,128)(2,1)} %near.3), channel_id=1, source_target_pairs={{0,24},{1,25},{2,26},{3,27},{4,28},{5,29},{6,30},{7,31},{8,16},{9,... | collective-permute-start | bytes 3145736 | tf_op jit(solution)/shard_map/ppermute | solution.py:22
  21.8 5.3 %collective-permute-start.2 = (bf16[2,64,1024]{2,1,0:T(8,128)(2,1)S(1)}, bf16[2,64,1024]{2,1,0:T(8,128)(2,1)S(1)}, u32[]{:S(2)}, u32[]{:S(2)}) collective-permute-start(bf16[2,64,1024]{2,1,0:T(8,128)(2,1)S(1)} %get-tuple-element.41), channel_id=1, source_target_pairs={{0,2},{1,3},{2,0},{3,1},{4,6},{5,7},{6,4},{7,5},{8,10},{9,11},{10,... | collective-permute-start | bytes 786440 | tf_op jit(solution)/shard_map/ppermute | solution.py:22
  27.9 7.8 %collective-permute-start.8 = (bf16[64,512]{1,0:T(8,128)(2,1)S(1)}, bf16[64,512]{1,0:T(8,128)(2,1)S(1)}, u32[]{:S(2)}, u32[]{:S(2)}) collective-permute-start(bf16[64,512]{1,0:T(8,128)(2,1)S(1)} %get-tuple-element.44), channel_id=1, source_target_pairs={{0,0},{1,1},{2,32},{3,33},{4,64},{5,65},{6,96},{7,97},{8,128},{9,1... | collective-permute-start | bytes 196616 | tf_op jit(solution)/shard_map/ppermute | solution.py:22
  35.8 6.3 %collective-permute-start.9 = (bf16[64,512]{1,0:T(8,128)(2,1)S(1)}, bf16[64,512]{1,0:T(8,128)(2,1)S(1)}, u32[]{:S(2)}, u32[]{:S(2)}) collective-permute-start(bf16[64,512]{1,0:T(8,128)(2,1)S(1)} %get-tuple-element.45), channel_id=1, source_target_pairs={{0,1},{1,0},{2,33},{3,32},{4,65},{5,64},{6,97},{7,96},{8,129},{9,1... | collective-permute-start | bytes 196616 | tf_op jit(solution)/shard_map/ppermute | solution.py:22
  42.1 1.8 %collective-permute-done.4.three = bf16[512,1024]{1,0:T(8,128)(2,1)S(1)} collective-permute-done((bf16[512,1024]{1,0:T(8,128)(2,1)}, bf16[512,1024]{1,0:T(8,128)(2,1)S(1)}, u32[]{:S(2)}, u32[]{:S(2)}) %collective-permute-start.4) | collective-permute-done | bytes 1048608 | tf_op jit(solution)/shard_map/ppermute | solution.py:22
  43.9 3.8 %collective-permute-start.5 = (bf16[2,2,64,1024]{3,2,0,1:T(8,128)(2,1)S(1)}, bf16[2,2,64,1024]{3,2,0,1:T(8,128)(2,1)S(1)}, u32[]{:S(2)}, u32[]{:S(2)}) collective-permute-start(bf16[2,2,64,1024]{3,2,0,1:T(8,128)(2,1)S(1)} %pad_maximum_fusion), channel_id=1, source_target_pairs={{0,1},{1,0},{2,3},{3,2},{4,5},{5,4},{6,7},{7,6},{8,9},{9,8},{10,11... | collective-permute-start | bytes 1572872 | tf_op jit(solution)/shard_map/ppermute | solution.py:22
  47.7 0.7 fusion.13
  48.4 7.0 %collective-permute-done.9 = bf16[64,512]{1,0:T(8,128)(2,1)S(1)} collective-permute-done((bf16[64,512]{1,0:T(8,128)(2,1)S(1)}, bf16[64,512]{1,0:T(8,128)(2,1)S(1)}, u32[]{:S(2)}, u32[]{:S(2)}) %collective-permute-start.9) | collective-permute-done | bytes 65568 | tf_op jit(solution)/shard_map/ppermute | solution.py:22
  55.6 2.7 %collective-permute-start.6 = (bf16[256,1024]{1,0:T(8,128)(2,1)S(1)}, bf16[256,1024]{1,0:T(8,128)(2,1)S(1)}, u32[]{:S(2)}, u32[]{:S(2)}) collective-permute-start(bf16[256,1024]{1,0:T(8,128)(2,1)S(1)} %slice.6), channel_id=1, source_target_pairs={{0,8},{1,9},{2,10},{3,11},{4,12},{5,13},{6,14},{7,15},{8,0},{9,1},... | collective-permute-start | bytes 1572872 | tf_op jit(solution)/shard_map/ppermute | solution.py:22
  58.4 2.9 %collective-permute-start.7 = (bf16[256,1024]{1,0:T(8,128)(2,1)S(1)}, bf16[256,1024]{1,0:T(8,128)(2,1)S(1)}, u32[]{:S(2)}, u32[]{:S(2)}) collective-permute-start(bf16[256,1024]{1,0:T(8,128)(2,1)S(1)} %slice.7), channel_id=1, source_target_pairs={{0,24},{1,25},{2,26},{3,27},{4,28},{5,29},{6,30},{7,31},{8,16},{9,... | collective-permute-start | bytes 1572872 | tf_op jit(solution)/shard_map/ppermute | solution.py:22
  61.8 5.2 %collective-permute-done.6.upper = bf16[256,1024]{1,0:T(8,128)(2,1)S(1)} collective-permute-done((bf16[256,1024]{1,0:T(8,128)(2,1)S(1)}, bf16[256,1024]{1,0:T(8,128)(2,1)S(1)}, u32[]{:S(2)}, u32[]{:S(2)}) %collective-permute-start.6) | collective-permute-done | bytes 524320 | tf_op jit(solution)/shard_map/ppermute | solution.py:22
  67.0 5.9 %collective-permute-done.7.lower = bf16[256,1024]{1,0:T(8,128)(2,1)S(1)} collective-permute-done((bf16[256,1024]{1,0:T(8,128)(2,1)S(1)}, bf16[256,1024]{1,0:T(8,128)(2,1)S(1)}, u32[]{:S(2)}, u32[]{:S(2)}) %collective-permute-start.7) | collective-permute-done | bytes 524320 | tf_op jit(solution)/shard_map/ppermute | solution.py:22
  72.9 1.3 shard_map.77
  74.2 1.9 %collective-permute-start.10 = (bf16[4,256,512]{2,1,0:T(8,128)(2,1)S(1)}, bf16[4,256,512]{2,1,0:T(8,128)(2,1)S(1)}, u32[]{:S(2)}, u32[]{:S(2)}) collective-permute-start(bf16[4,256,512]{2,1,0:T(8,128)(2,1)S(1)} %shard_map.77), channel_id=1, source_target_pairs={{0,32},{1,33},{2,34},{3,35},{4,36},{5,37},{6,38},{7,39},{8,40},{9,... | collective-permute-start | bytes 3145736 | tf_op jit(solution)/shard_map/ppermute | solution.py:22
  76.1 2.6 %collective-permute-done.10.rest_0_ = bf16[4,256,512]{2,1,0:T(8,128)(2,1)S(1)} collective-permute-done((bf16[4,256,512]{2,1,0:T(8,128)(2,1)S(1)}, bf16[4,256,512]{2,1,0:T(8,128)(2,1)S(1)}, u32[]{:S(2)}, u32[]{:S(2)}) %collective-permute-start.10) | collective-permute-done | bytes 1048608 | tf_op jit(solution)/shard_map/ppermute | solution.py:22
  78.8 2.3 %shard_map.78 = bf16[4,256,512]{2,1,0:T(8,128)(2,1)} custom-call(bf16[256,1024]{1,0:T(8,128)(2,1)S(1)} %bitcast.30, bf16[512,1024]{1,0:T(8,128)(2,1)S(1)} %copy-done, bf16[512,1024]{1,0:T(8,128)(2,1)S(1)} %collective-permute-done.3.one, bf16[256,1024]{1,0:T(8,128)(2,1)S(1)} %collective-permute-done.6.upper, ...), custom_call_target="tpu_custom_call" | custom-call | flops 1073741824 | bytes 5767168 | tf_op jit(solution)/shard_map/pallas_call | solution.py:69
  81.0 10.4 %all-to-all-start = ((bf16[4,256,512]{2,1,0:T(8,128)(2,1)}), bf16[4,256,512]{2,1,0:T(8,128)(2,1)S(1)}, u32[]{:S(2)}, u32[]{:S(2)}) async-start(bf16[4,256,512]{2,1,0:T(8,128)(2,1)} %shard_map.78), calls=%async_computation | async-start | bytes 2097152 | tf_op jit(solution)/shard_map/all_to_all | solution.py:159
  91.4 1.9 %collective-permute-start.13 = (bf16[128,512]{1,0:T(8,128)(2,1)S(1)}, bf16[128,512]{1,0:T(8,128)(2,1)S(1)}, u32[]{:S(2)}, u32[]{:S(2)}) collective-permute-start(bf16[128,512]{1,0:T(8,128)(2,1)S(1)} %fusion.9), channel_id=1, source_target_pairs={{0,32},{1,33},{2,34},{3,35},{4,36},{5,37},{6,38},{7,39},{8,40},{9,... | collective-permute-start | bytes 393224 | tf_op jit(solution)/shard_map/ppermute | solution.py:22
  93.3 11.4 %all-to-all-done = bf16[4,256,512]{2,1,0:T(8,128)(2,1)S(1)} async-done(((bf16[4,256,512]{2,1,0:T(8,128)(2,1)}), bf16[4,256,512]{2,1,0:T(8,128)(2,1)S(1)}, u32[]{:S(2)}, u32[]{:S(2)}) %all-to-all-start) | async-done | bytes 1048608 | tf_op jit(solution)/shard_map/all_to_all | solution.py:159
  105.0 12.7 %collective-permute-start.12 = (bf16[128,512]{1,0:T(8,128)(2,1)S(1)}, bf16[128,512]{1,0:T(8,128)(2,1)S(1)}, u32[]{:S(2)}, u32[]{:S(2)}) collective-permute-start(bf16[128,512]{1,0:T(8,128)(2,1)S(1)} %get-tuple-element.39), channel_id=1, source_target_pairs={{0,256},{1,257},{2,258},{3,259},{4,260},{5,261},{6,262},{7,263},{8... | collective-permute-start | bytes 393224 | tf_op jit(solution)/shard_map/ppermute | solution.py:22
  117.7 6.2 %collective-permute-start.11 = (bf16[128,512]{1,0:T(8,128)(2,1)S(1)}, bf16[128,512]{1,0:T(8,128)(2,1)S(1)}, u32[]{:S(2)}, u32[]{:S(2)}) collective-permute-start(bf16[128,512]{1,0:T(8,128)(2,1)S(1)} %get-tuple-element.38), channel_id=1, source_target_pairs={{0,0},{1,1},{2,2},{3,3},{4,4},{5,5},{6,6},{7,7},{8,64},{9,65},{10,... | collective-permute-start | bytes 393224 | tf_op jit(solution)/shard_map/ppermute | solution.py:22
  124.0 2.8 %collective-permute-done.12 = bf16[128,512]{1,0:T(8,128)(2,1)S(1)} collective-permute-done((bf16[128,512]{1,0:T(8,128)(2,1)S(1)}, bf16[128,512]{1,0:T(8,128)(2,1)S(1)}, u32[]{:S(2)}, u32[]{:S(2)}) %collective-permute-start.12) | collective-permute-done | bytes 131104 | tf_op jit(solution)/shard_map/ppermute | solution.py:22
  126.8 6.0 %collective-permute-done.11 = bf16[128,512]{1,0:T(8,128)(2,1)S(1)} collective-permute-done((bf16[128,512]{1,0:T(8,128)(2,1)S(1)}, bf16[128,512]{1,0:T(8,128)(2,1)S(1)}, u32[]{:S(2)}, u32[]{:S(2)}) %collective-permute-start.11) | collective-permute-done | bytes 131104 | tf_op jit(solution)/shard_map/ppermute | solution.py:22
  133.0 23.2 %all_to_all.15 = bf16[32,8,128]{2,1,0:T(8,128)(2,1)S(1)} all-to-all(bf16[32,8,128]{2,1,0:T(8,128)(2,1)S(1)} %fusion), channel_id=1, replica_groups=mesh['prow'=16,'pcol'=32] {'pcol'}, dimensions={0} | all-to-all | bytes 131072 | tf_op jit(solution)/shard_map/all_to_all | solution.py:171
  156.9 3.9 %all-to-all-start.2 = ((bf16[32,8,128]{2,1,0:T(8,128)(2,1)}), bf16[32,8,128]{2,1,0:T(8,128)(2,1)S(1)}, u32[]{:S(2)}, u32[]{:S(2)}) async-start(bf16[32,8,128]{2,1,0:T(8,128)(2,1)} %broadcast_in_dim.88), calls=%async_computation.2 | async-start | bytes 131072 | tf_op jit(solution)/shard_map/all_to_all | solution.py:173
  160.8 0.7 iota_compare_fusion.3
  161.6 0.8 copy.17
  162.4 11.1 %all-to-all-done.2 = bf16[32,8,128]{2,1,0:T(8,128)(2,1)S(1)} async-done(((bf16[32,8,128]{2,1,0:T(8,128)(2,1)}), bf16[32,8,128]{2,1,0:T(8,128)(2,1)S(1)}, u32[]{:S(2)}, u32[]{:S(2)}) %all-to-all-start.2) | async-done | bytes 65568 | tf_op jit(solution)/shard_map/all_to_all | solution.py:173
  173.5 0.8 convert_add_fusion.1
  (63 shorter events, 5.5 us)
Async XLA Ops:
  0.6 18.4 %copy-start.3 = (s32[8,40]{1,0:T(8,128)S(1)}, s32[8,40]{1,0:T(8,128)}, u32[]{:S(2)}) copy-start(s32[8,40]{1,0:T(8,128)} %param.9) | copy-start | bytes 3844
  0.6 21.1 %collective-permute-start = (bf16[64,1024]{1,0:T(8,128)(2,1)}, bf16[64,1024]{1,0:T(8,128)(2,1)S(1)}, u32[]{:S(2)}, u32[]{:S(2)}) collective-permute-start(bf16[64,1024]{1,0:T(8,128)(2,1)} %bitcast.34), channel_id=1, source_target_pairs={{0,0},{1,1},{2,2},{3,3},{4,8},{5,9},{6,10},{7,11},{8,16},{9,17},{1... | collective-permute-start | bytes 393224 | tf_op jit(solution)/shard_map/ppermute | solution.py:22
  2.2 19.6 %collective-permute-start.1 = (bf16[64,1024]{1,0:T(8,128)(2,1)}, bf16[64,1024]{1,0:T(8,128)(2,1)S(1)}, u32[]{:S(2)}, u32[]{:S(2)}) collective-permute-start(bf16[64,1024]{1,0:T(8,128)(2,1)} %bitcast.35), channel_id=1, source_target_pairs={{0,4},{1,5},{2,6},{3,7},{4,12},{5,13},{6,14},{7,15},{8,20},{9,21},... | collective-permute-start | bytes 393224 | tf_op jit(solution)/shard_map/ppermute | solution.py:22
  11.7 30.4 %collective-permute-start.3 = (bf16[512,1024]{1,0:T(8,128)(2,1)}, bf16[512,1024]{1,0:T(8,128)(2,1)S(1)}, u32[]{:S(2)}, u32[]{:S(2)}) collective-permute-start(bf16[512,1024]{1,0:T(8,128)(2,1)} %near.3), channel_id=1, source_target_pairs={{0,8},{1,9},{2,10},{3,11},{4,12},{5,13},{6,14},{7,15},{8,0},{9,1},... | collective-permute-start | bytes 3145736 | tf_op jit(solution)/shard_map/ppermute | solution.py:22
  16.5 27.4 %collective-permute-start.4 = (bf16[512,1024]{1,0:T(8,128)(2,1)}, bf16[512,1024]{1,0:T(8,128)(2,1)S(1)}, u32[]{:S(2)}, u32[]{:S(2)}) collective-permute-start(bf16[512,1024]{1,0:T(8,128)(2,1)} %near.3), channel_id=1, source_target_pairs={{0,24},{1,25},{2,26},{3,27},{4,28},{5,29},{6,30},{7,31},{8,16},{9,... | collective-permute-start | bytes 3145736 | tf_op jit(solution)/shard_map/ppermute | solution.py:22
  19.1 0.7 copy-start.4
  20.9 0.7 copy-start.5
  21.8 6.1 %copy-start.1 = (bf16[1024,64]{0,1:T(8,128)(2,1)S(1)}, bf16[1024,64]{0,1:T(8,128)(2,1)}, u32[]{:S(2)}) copy-start(bf16[1024,64]{0,1:T(8,128)(2,1)} %param.7) | copy-start | bytes 393220
  21.8 20.2 %collective-permute-start.2 = (bf16[2,64,1024]{2,1,0:T(8,128)(2,1)S(1)}, bf16[2,64,1024]{2,1,0:T(8,128)(2,1)S(1)}, u32[]{:S(2)}, u32[]{:S(2)}) collective-permute-start(bf16[2,64,1024]{2,1,0:T(8,128)(2,1)S(1)} %get-tuple-element.41), channel_id=1, source_target_pairs={{0,2},{1,3},{2,0},{3,1},{4,6},{5,7},{6,4},{7,5},{8,10},{9,11},{10,... | collective-permute-start | bytes 786440 | tf_op jit(solution)/shard_map/ppermute | solution.py:22
  27.9 20.5 %collective-permute-start.8 = (bf16[64,512]{1,0:T(8,128)(2,1)S(1)}, bf16[64,512]{1,0:T(8,128)(2,1)S(1)}, u32[]{:S(2)}, u32[]{:S(2)}) collective-permute-start(bf16[64,512]{1,0:T(8,128)(2,1)S(1)} %get-tuple-element.44), channel_id=1, source_target_pairs={{0,0},{1,1},{2,32},{3,33},{4,64},{5,65},{6,96},{7,97},{8,128},{9,1... | collective-permute-start | bytes 196616 | tf_op jit(solution)/shard_map/ppermute | solution.py:22
  35.8 19.7 %collective-permute-start.9 = (bf16[64,512]{1,0:T(8,128)(2,1)S(1)}, bf16[64,512]{1,0:T(8,128)(2,1)S(1)}, u32[]{:S(2)}, u32[]{:S(2)}) collective-permute-start(bf16[64,512]{1,0:T(8,128)(2,1)S(1)} %get-tuple-element.45), channel_id=1, source_target_pairs={{0,1},{1,0},{2,33},{3,32},{4,65},{5,64},{6,97},{7,96},{8,129},{9,1... | collective-permute-start | bytes 196616 | tf_op jit(solution)/shard_map/ppermute | solution.py:22
  43.9 17.4 %collective-permute-start.5 = (bf16[2,2,64,1024]{3,2,0,1:T(8,128)(2,1)S(1)}, bf16[2,2,64,1024]{3,2,0,1:T(8,128)(2,1)S(1)}, u32[]{:S(2)}, u32[]{:S(2)}) collective-permute-start(bf16[2,2,64,1024]{3,2,0,1:T(8,128)(2,1)S(1)} %pad_maximum_fusion), channel_id=1, source_target_pairs={{0,1},{1,0},{2,3},{3,2},{4,5},{5,4},{6,7},{7,6},{8,9},{9,8},{10,11... | collective-permute-start | bytes 1572872 | tf_op jit(solution)/shard_map/ppermute | solution.py:22
  55.6 11.4 %collective-permute-start.6 = (bf16[256,1024]{1,0:T(8,128)(2,1)S(1)}, bf16[256,1024]{1,0:T(8,128)(2,1)S(1)}, u32[]{:S(2)}, u32[]{:S(2)}) collective-permute-start(bf16[256,1024]{1,0:T(8,128)(2,1)S(1)} %slice.6), channel_id=1, source_target_pairs={{0,8},{1,9},{2,10},{3,11},{4,12},{5,13},{6,14},{7,15},{8,0},{9,1},... | collective-permute-start | bytes 1572872 | tf_op jit(solution)/shard_map/ppermute | solution.py:22
  58.4 14.6 %collective-permute-start.7 = (bf16[256,1024]{1,0:T(8,128)(2,1)S(1)}, bf16[256,1024]{1,0:T(8,128)(2,1)S(1)}, u32[]{:S(2)}, u32[]{:S(2)}) collective-permute-start(bf16[256,1024]{1,0:T(8,128)(2,1)S(1)} %slice.7), channel_id=1, source_target_pairs={{0,24},{1,25},{2,26},{3,27},{4,28},{5,29},{6,30},{7,31},{8,16},{9,... | collective-permute-start | bytes 1572872 | tf_op jit(solution)/shard_map/ppermute | solution.py:22
  61.7 11.2 %copy-start = (bf16[512,1024]{1,0:T(8,128)(2,1)S(1)}, bf16[512,1024]{1,0:T(8,128)(2,1)}, u32[]{:S(2)}) copy-start(bf16[512,1024]{1,0:T(8,128)(2,1)} %near.3) | copy-start | bytes 3145732
  74.2 4.6 %collective-permute-start.10 = (bf16[4,256,512]{2,1,0:T(8,128)(2,1)S(1)}, bf16[4,256,512]{2,1,0:T(8,128)(2,1)S(1)}, u32[]{:S(2)}, u32[]{:S(2)}) collective-permute-start(bf16[4,256,512]{2,1,0:T(8,128)(2,1)S(1)} %shard_map.77), channel_id=1, source_target_pairs={{0,32},{1,33},{2,34},{3,35},{4,36},{5,37},{6,38},{7,39},{8,40},{9,... | collective-permute-start | bytes 3145736 | tf_op jit(solution)/shard_map/ppermute | solution.py:22
  81.0 23.7 %all-to-all-start = ((bf16[4,256,512]{2,1,0:T(8,128)(2,1)}), bf16[4,256,512]{2,1,0:T(8,128)(2,1)S(1)}, u32[]{:S(2)}, u32[]{:S(2)}) async-start(bf16[4,256,512]{2,1,0:T(8,128)(2,1)} %shard_map.78), calls=%async_computation | async-start | bytes 2097152 | tf_op jit(solution)/shard_map/all_to_all | solution.py:159
  91.4 32.5 %collective-permute-start.13 = (bf16[128,512]{1,0:T(8,128)(2,1)S(1)}, bf16[128,512]{1,0:T(8,128)(2,1)S(1)}, u32[]{:S(2)}, u32[]{:S(2)}) collective-permute-start(bf16[128,512]{1,0:T(8,128)(2,1)S(1)} %fusion.9), channel_id=1, source_target_pairs={{0,32},{1,33},{2,34},{3,35},{4,36},{5,37},{6,38},{7,39},{8,40},{9,... | collective-permute-start | bytes 393224 | tf_op jit(solution)/shard_map/ppermute | solution.py:22
  105.0 21.7 %collective-permute-start.12 = (bf16[128,512]{1,0:T(8,128)(2,1)S(1)}, bf16[128,512]{1,0:T(8,128)(2,1)S(1)}, u32[]{:S(2)}, u32[]{:S(2)}) collective-permute-start(bf16[128,512]{1,0:T(8,128)(2,1)S(1)} %get-tuple-element.39), channel_id=1, source_target_pairs={{0,256},{1,257},{2,258},{3,259},{4,260},{5,261},{6,262},{7,263},{8... | collective-permute-start | bytes 393224 | tf_op jit(solution)/shard_map/ppermute | solution.py:22
  117.7 15.0 %collective-permute-start.11 = (bf16[128,512]{1,0:T(8,128)(2,1)S(1)}, bf16[128,512]{1,0:T(8,128)(2,1)S(1)}, u32[]{:S(2)}, u32[]{:S(2)}) collective-permute-start(bf16[128,512]{1,0:T(8,128)(2,1)S(1)} %get-tuple-element.38), channel_id=1, source_target_pairs={{0,0},{1,1},{2,2},{3,3},{4,4},{5,5},{6,6},{7,7},{8,64},{9,65},{10,... | collective-permute-start | bytes 393224 | tf_op jit(solution)/shard_map/ppermute | solution.py:22
  156.9 16.6 %all-to-all-start.2 = ((bf16[32,8,128]{2,1,0:T(8,128)(2,1)}), bf16[32,8,128]{2,1,0:T(8,128)(2,1)S(1)}, u32[]{:S(2)}, u32[]{:S(2)}) async-start(bf16[32,8,128]{2,1,0:T(8,128)(2,1)} %broadcast_in_dim.88), calls=%async_computation.2 | async-start | bytes 131072 | tf_op jit(solution)/shard_map/all_to_all | solution.py:173
  161.6 11.8 %copy-start.2 = (f32[256,128]{1,0:T(8,128)S(1)}, f32[256,128]{1,0:T(8,128)}, u32[]{:S(2)}) copy-start(f32[256,128]{1,0:T(8,128)} %param.8) | copy-start | bytes 393220

commit v5 on v4

--- a/solution.py
+++ b/solution.py
@@ -86,6 +86,23 @@
     x, zl = pcol >> 3, pcol & 7
     high, mid, low = zl >> 2, (zl >> 1) & 1, zl & 1
 
+    slots = jnp.arange(rowblocks.shape[1], dtype=jnp.int32)
+    used = jnp.where(slots[None, :] < counts[:, None], rowblocks, -1)
+    member = jnp.any(used[:, :, None] == jnp.arange(64, dtype=jnp.int32)[None, None, :], axis=1)
+    nodes = jnp.arange(SNODES, dtype=jnp.int32)
+    my_nodes = (high ^ jnp.arange(2, dtype=jnp.int32)) * 4 + x
+    chosen = my_nodes[:, None] == nodes[None, :]
+    my_blocks = prow * 4 + jnp.arange(4, dtype=jnp.int32)
+    block_is = my_blocks[:, None] == jnp.arange(64, dtype=jnp.int32)[None, :]
+    live = jnp.any(
+        chosen[:, None, :, None] & block_is[None, :, None, :] & member[None, None, :, :], axis=(2, 3)
+    )
+    width = jnp.sum(jnp.where(chosen, widths[None, :], 0), axis=1)
+    half_of = (mid ^ jnp.arange(2, dtype=jnp.int32))[:, None] * 128
+    within = half_of + low * 64 + jnp.arange(64, dtype=jnp.int32)[None, :]
+    active = (within[None] < width[:, None, None]).astype(jnp.bfloat16)
+    row_scale = jnp.repeat(live.astype(jnp.bfloat16), B, axis=1)
+
     own = lpanel.T
     first = send(own, lambda *d: fold_x(*d, 0))
     second = send(own, lambda *d: fold_x(*d, 1))
@@ -101,8 +118,8 @@
     near = send(pair, lambda zh, y, core, x, zl: (zh, y, core, x, zl ^ 2))
     a1 = send(ainv, lambda zh, y, core, x, zl: (zh, y, core, x ^ 1, zl))
     a3 = send(ainv, lambda zh, y, core, x, zl: (zh, y, core, x ^ 3, zl))
-    quad = jnp.stack([pair, near], axis=1)
-    quad, a1, a3 = lax.optimization_barrier((quad, a1, a3))
+    near, a1, a3 = lax.optimization_barrier((near, a1, a3))
+    quad = jnp.stack([pair, near], axis=1) * active[..., None] * row_scale[:, None, None, :]
     last = send(quad, lambda zh, y, core, x, zl: (zh, y, core, x, zl ^ 1))
 
     half = ainv.shape[0] // 2
@@ -110,22 +127,6 @@
         send(a3[:half], lambda zh, y, core, x, zl: (zh, y, core, x ^ 1, zl)),
         send(a1[half:], lambda zh, y, core, x, zl: (zh, y, core, x ^ 3, zl)),
     ]
-
-    slots = jnp.arange(rowblocks.shape[1], dtype=jnp.int32)
-    used = jnp.where(slots[None, :] < counts[:, None], rowblocks, -1)
-    member = jnp.any(used[:, :, None] == jnp.arange(64, dtype=jnp.int32)[None, None, :], axis=1)
-    nodes = jnp.arange(SNODES, dtype=jnp.int32)
-    my_nodes = (high ^ jnp.arange(2, dtype=jnp.int32)) * 4 + x
-    chosen = my_nodes[:, None] == nodes[None, :]
-    my_blocks = prow * 4 + jnp.arange(4, dtype=jnp.int32)
-    block_is = my_blocks[:, None] == jnp.arange(64, dtype=jnp.int32)[None, :]
-    live = jnp.any(
-        chosen[:, None, :, None] & block_is[None, :, None, :] & member[None, None, :, :], axis=(2, 3)
-    )
-    width = jnp.sum(jnp.where(chosen, widths[None, :], 0), axis=1)
-    half_of = (mid ^ jnp.arange(2, dtype=jnp.int32))[:, None, None] * 128
-    within = half_of + jnp.arange(128, dtype=jnp.int32).reshape(1, 2, 64)
-    active = within[None] < width[:, None, None, None]
 
     node = prow >> 1
     row_ids = pcol * 2 + jnp.arange(2, dtype=jnp.int32)
@@ -144,9 +145,6 @@
     factor = jnp.stack(
         [jnp.where(low == 0, quad, last), jnp.where(low == 0, last, quad)], axis=2
     )
-    row_scale = jnp.repeat(live.astype(jnp.bfloat16), B, axis=1)
-    factor = factor * active[..., None].astype(jnp.bfloat16) * row_scale[:, None, None, None, :]
-
     keep = core ^ mid
     theirs = lax.dynamic_index_in_dim(factor, 1 - keep, 1, keepdims=False).reshape(256, 1024)
     ours = lax.dynamic_index_in_dim(factor, keep, 1, keepdims=False).reshape(256, 1024)

time: 175 us -> 176 us (level)
  no operation moved by 1% of the time
where the time goes in v5:
time: 176 us; the launch traced here: 174 us
  starting transfers between devices  84.2 us (48%)
  waiting for transfers between devices  54 us (31%)
  blocking collectives  23.3 us (13%)
  other arithmetic  4.86 us (3%)
  Pallas kernels  3.54 us (2%)
  local copies, waits for them, and re-layouts  2.98 us (2%)
    ppermute x14, starting transfers between devices, send(): return lax.ppermute(value, AXES, pairs)  71.1 us
    ppermute x14, waiting for transfers between devices, send(): return lax.ppermute(value, AXES, pairs)  31.5 us
    all_to_all x1, blocking collectives, per_device(): pieces = lax.all_to_all(terms.reshape(32, 8, 128), 'pcol', 0, 0)  23.3 us
    all_to_all x1, waiting for transfers between devices, per_device(): shares = lax.all_to_all(chip, AXES, 0, 0, axis_index_groups=swap_groups())  11.4 us
    all_to_all x1, waiting for transfers between devices, per_device(): lax.all_to_all(jnp.broadcast_to(piece[None], (32, 8, 128)), 'pcol', 0, 0)  11.1 us
    all_to_all x1, starting transfers between devices, per_device(): shares = lax.all_to_all(chip, AXES, 0, 0, axis_index_groups=swap_groups())  9.26 us
    all_to_all x1, starting transfers between devices, per_device(): lax.all_to_all(jnp.broadcast_to(piece[None], (32, 8, 128)), 'pcol', 0, 0)  3.92 us
    pallas_call x2, Pallas kernels, partial_product(): pl.pallas_call(functools.partial(product_kernel, len(added)), in_specs=[p...  3.54 us
  transfers between devices with their start and end apart: 16, of which 9 were waited for; matrix products, arithmetic and copies ran while one was open for 3% of the time, Pallas kernels for 0%

profile of v5, /device:TPU:24, one launch (start us, length us, event | category | flops | bytes accessed | tf_op | source)
XLA Modules:
  0.0 174.2 jit_solution(3327988435192633562)
XLA Ops:
  0.6 1.6 collective-permute-start
  2.2 9.5 %collective-permute-start.1 = (bf16[64,1024]{1,0:T(8,128)(2,1)}, bf16[64,1024]{1,0:T(8,128)(2,1)S(1)}, u32[]{:S(2)}, u32[]{:S(2)}) collective-permute-start(bf16[64,1024]{1,0:T(8,128)(2,1)} %bitcast.36), channel_id=1, source_target_pairs={{0,4},{1,5},{2,6},{3,7},{4,12},{5,13},{6,14},{7,15},{8,20},{9,21},... | collective-permute-start | bytes 393224 | tf_op jit(solution)/shard_map/ppermute | solution.py:22
  11.7 4.9 %collective-permute-start.3 = (bf16[512,1024]{1,0:T(8,128)(2,1)}, bf16[512,1024]{1,0:T(8,128)(2,1)S(1)}, u32[]{:S(2)}, u32[]{:S(2)}) collective-permute-start(bf16[512,1024]{1,0:T(8,128)(2,1)} %near.3), channel_id=1, source_target_pairs={{0,8},{1,9},{2,10},{3,11},{4,12},{5,13},{6,14},{7,15},{8,0},{9,1},... | collective-permute-start | bytes 3145736 | tf_op jit(solution)/shard_map/ppermute | solution.py:22
  16.5 2.5 %collective-permute-start.4 = (bf16[512,1024]{1,0:T(8,128)(2,1)}, bf16[512,1024]{1,0:T(8,128)(2,1)S(1)}, u32[]{:S(2)}, u32[]{:S(2)}) collective-permute-start(bf16[512,1024]{1,0:T(8,128)(2,1)} %near.3), channel_id=1, source_target_pairs={{0,24},{1,25},{2,26},{3,27},{4,28},{5,29},{6,30},{7,31},{8,16},{9,... | collective-permute-start | bytes 3145736 | tf_op jit(solution)/shard_map/ppermute | solution.py:22
  19.1 0.7 copy-done.3
  21.6 5.3 %collective-permute-start.2 = (bf16[2,64,1024]{2,1,0:T(8,128)(2,1)S(1)}, bf16[2,64,1024]{2,1,0:T(8,128)(2,1)S(1)}, u32[]{:S(2)}, u32[]{:S(2)}) collective-permute-start(bf16[2,64,1024]{2,1,0:T(8,128)(2,1)S(1)} %get-tuple-element.41), channel_id=1, source_target_pairs={{0,2},{1,3},{2,0},{3,1},{4,6},{5,7},{6,4},{7,5},{8,10},{9,11},{10,... | collective-permute-start | bytes 786440 | tf_op jit(solution)/shard_map/ppermute | solution.py:22
  27.7 7.8 %collective-permute-start.8 = (bf16[64,512]{1,0:T(8,128)(2,1)S(1)}, bf16[64,512]{1,0:T(8,128)(2,1)S(1)}, u32[]{:S(2)}, u32[]{:S(2)}) collective-permute-start(bf16[64,512]{1,0:T(8,128)(2,1)S(1)} %get-tuple-element.44), channel_id=1, source_target_pairs={{0,0},{1,1},{2,32},{3,33},{4,64},{5,65},{6,96},{7,97},{8,128},{9,1... | collective-permute-start | bytes 196616 | tf_op jit(solution)/shard_map/ppermute | solution.py:22
  35.6 6.5 %collective-permute-start.9 = (bf16[64,512]{1,0:T(8,128)(2,1)S(1)}, bf16[64,512]{1,0:T(8,128)(2,1)S(1)}, u32[]{:S(2)}, u32[]{:S(2)}) collective-permute-start(bf16[64,512]{1,0:T(8,128)(2,1)S(1)} %get-tuple-element.45), channel_id=1, source_target_pairs={{0,1},{1,0},{2,33},{3,32},{4,65},{5,64},{6,97},{7,96},{8,129},{9,1... | collective-permute-start | bytes 196616 | tf_op jit(solution)/shard_map/ppermute | solution.py:22
  42.0 1.9 %collective-permute-done.4.three = bf16[512,1024]{1,0:T(8,128)(2,1)S(1)} collective-permute-done((bf16[512,1024]{1,0:T(8,128)(2,1)}, bf16[512,1024]{1,0:T(8,128)(2,1)S(1)}, u32[]{:S(2)}, u32[]{:S(2)}) %collective-permute-start.4) | collective-permute-done | bytes 1048608 | tf_op jit(solution)/shard_map/ppermute | solution.py:22
  44.0 3.8 %collective-permute-start.5 = (bf16[2,2,64,1024]{3,2,0,1:T(8,128)(2,1)S(1)}, bf16[2,2,64,1024]{3,2,0,1:T(8,128)(2,1)S(1)}, u32[]{:S(2)}, u32[]{:S(2)}) collective-permute-start(bf16[2,2,64,1024]{3,2,0,1:T(8,128)(2,1)S(1)} %fusion.3), channel_id=1, source_target_pairs={{0,1},{1,0},{2,3},{3,2},{4,5},{5,4},{6,7},{7,6},{8,9},{9,8},{10,11... | collective-permute-start | bytes 1572872 | tf_op jit(solution)/shard_map/ppermute | solution.py:22
  47.9 0.7 fusion.15
  48.5 6.0 %collective-permute-done.9 = bf16[64,512]{1,0:T(8,128)(2,1)S(1)} collective-permute-done((bf16[64,512]{1,0:T(8,128)(2,1)S(1)}, bf16[64,512]{1,0:T(8,128)(2,1)S(1)}, u32[]{:S(2)}, u32[]{:S(2)}) %collective-permute-start.9) | collective-permute-done | bytes 65568 | tf_op jit(solution)/shard_map/ppermute | solution.py:22
  54.6 3.4 %collective-permute-start.6 = (bf16[256,1024]{1,0:T(8,128)(2,1)S(1)}, bf16[256,1024]{1,0:T(8,128)(2,1)S(1)}, u32[]{:S(2)}, u32[]{:S(2)}) collective-permute-start(bf16[256,1024]{1,0:T(8,128)(2,1)S(1)} %slice.6), channel_id=1, source_target_pairs={{0,8},{1,9},{2,10},{3,11},{4,12},{5,13},{6,14},{7,15},{8,0},{9,1},... | collective-permute-start | bytes 1572872 | tf_op jit(solution)/shard_map/ppermute | solution.py:22
  58.1 2.9 %collective-permute-start.7 = (bf16[256,1024]{1,0:T(8,128)(2,1)S(1)}, bf16[256,1024]{1,0:T(8,128)(2,1)S(1)}, u32[]{:S(2)}, u32[]{:S(2)}) collective-permute-start(bf16[256,1024]{1,0:T(8,128)(2,1)S(1)} %slice.7), channel_id=1, source_target_pairs={{0,24},{1,25},{2,26},{3,27},{4,28},{5,29},{6,30},{7,31},{8,16},{9,... | collective-permute-start | bytes 1572872 | tf_op jit(solution)/shard_map/ppermute | solution.py:22
  61.5 5.2 %collective-permute-done.6.upper = bf16[256,1024]{1,0:T(8,128)(2,1)S(1)} collective-permute-done((bf16[256,1024]{1,0:T(8,128)(2,1)S(1)}, bf16[256,1024]{1,0:T(8,128)(2,1)S(1)}, u32[]{:S(2)}, u32[]{:S(2)}) %collective-permute-start.6) | collective-permute-done | bytes 524320 | tf_op jit(solution)/shard_map/ppermute | solution.py:22
  66.7 7.2 %collective-permute-done.7.lower = bf16[256,1024]{1,0:T(8,128)(2,1)S(1)} collective-permute-done((bf16[256,1024]{1,0:T(8,128)(2,1)S(1)}, bf16[256,1024]{1,0:T(8,128)(2,1)S(1)}, u32[]{:S(2)}, u32[]{:S(2)}) %collective-permute-start.7) | collective-permute-done | bytes 524320 | tf_op jit(solution)/shard_map/ppermute | solution.py:22
  73.9 1.3 shard_map.77
  75.2 1.9 %collective-permute-start.10 = (bf16[4,256,512]{2,1,0:T(8,128)(2,1)S(1)}, bf16[4,256,512]{2,1,0:T(8,128)(2,1)S(1)}, u32[]{:S(2)}, u32[]{:S(2)}) collective-permute-start(bf16[4,256,512]{2,1,0:T(8,128)(2,1)S(1)} %shard_map.77), channel_id=1, source_target_pairs={{0,32},{1,33},{2,34},{3,35},{4,36},{5,37},{6,38},{7,39},{8,40},{9,... | collective-permute-start | bytes 3145736 | tf_op jit(solution)/shard_map/ppermute | solution.py:22
  77.2 2.6 %collective-permute-done.10.rest_0_ = bf16[4,256,512]{2,1,0:T(8,128)(2,1)S(1)} collective-permute-done((bf16[4,256,512]{2,1,0:T(8,128)(2,1)S(1)}, bf16[4,256,512]{2,1,0:T(8,128)(2,1)S(1)}, u32[]{:S(2)}, u32[]{:S(2)}) %collective-permute-start.10) | collective-permute-done | bytes 1048608 | tf_op jit(solution)/shard_map/ppermute | solution.py:22
  79.8 2.3 %shard_map.78 = bf16[4,256,512]{2,1,0:T(8,128)(2,1)} custom-call(bf16[256,1024]{1,0:T(8,128)(2,1)S(1)} %bitcast.30, bf16[512,1024]{1,0:T(8,128)(2,1)S(1)} %copy-done, bf16[512,1024]{1,0:T(8,128)(2,1)S(1)} %collective-permute-done.3.one, bf16[256,1024]{1,0:T(8,128)(2,1)S(1)} %collective-permute-done.6.upper, ...), custom_call_target="tpu_custom_call" | custom-call | flops 1073741824 | bytes 5767168 | tf_op jit(solution)/shard_map/pallas_call | solution.py:69
  82.0 9.3 %all-to-all-start = ((bf16[4,256,512]{2,1,0:T(8,128)(2,1)}), bf16[4,256,512]{2,1,0:T(8,128)(2,1)S(1)}, u32[]{:S(2)}, u32[]{:S(2)}) async-start(bf16[4,256,512]{2,1,0:T(8,128)(2,1)} %shard_map.78), calls=%async_computation | async-start | bytes 2097152 | tf_op jit(solution)/shard_map/all_to_all | solution.py:157
  91.3 1.9 %collective-permute-start.13 = (bf16[128,512]{1,0:T(8,128)(2,1)S(1)}, bf16[128,512]{1,0:T(8,128)(2,1)S(1)}, u32[]{:S(2)}, u32[]{:S(2)}) collective-permute-start(bf16[128,512]{1,0:T(8,128)(2,1)S(1)} %fusion.11), channel_id=1, source_target_pairs={{0,32},{1,33},{2,34},{3,35},{4,36},{5,37},{6,38},{7,39},{8,40},{9,... | collective-permute-start | bytes 393224 | tf_op jit(solution)/shard_map/ppermute | solution.py:22
  93.2 11.4 %all-to-all-done = bf16[4,256,512]{2,1,0:T(8,128)(2,1)S(1)} async-done(((bf16[4,256,512]{2,1,0:T(8,128)(2,1)}), bf16[4,256,512]{2,1,0:T(8,128)(2,1)S(1)}, u32[]{:S(2)}, u32[]{:S(2)}) %all-to-all-start) | async-done | bytes 1048608 | tf_op jit(solution)/shard_map/all_to_all | solution.py:157
  104.9 12.9 %collective-permute-start.12 = (bf16[128,512]{1,0:T(8,128)(2,1)S(1)}, bf16[128,512]{1,0:T(8,128)(2,1)S(1)}, u32[]{:S(2)}, u32[]{:S(2)}) collective-permute-start(bf16[128,512]{1,0:T(8,128)(2,1)S(1)} %get-tuple-element.39), channel_id=1, source_target_pairs={{0,256},{1,257},{2,258},{3,259},{4,260},{5,261},{6,262},{7,263},{8... | collective-permute-start | bytes 393224 | tf_op jit(solution)/shard_map/ppermute | solution.py:22
  117.8 6.2 %collective-permute-start.11 = (bf16[128,512]{1,0:T(8,128)(2,1)S(1)}, bf16[128,512]{1,0:T(8,128)(2,1)S(1)}, u32[]{:S(2)}, u32[]{:S(2)}) collective-permute-start(bf16[128,512]{1,0:T(8,128)(2,1)S(1)} %get-tuple-element.38), channel_id=1, source_target_pairs={{0,0},{1,1},{2,2},{3,3},{4,4},{5,5},{6,6},{7,7},{8,64},{9,65},{10,... | collective-permute-start | bytes 393224 | tf_op jit(solution)/shard_map/ppermute | solution.py:22
  124.0 2.6 %collective-permute-done.12 = bf16[128,512]{1,0:T(8,128)(2,1)S(1)} collective-permute-done((bf16[128,512]{1,0:T(8,128)(2,1)S(1)}, bf16[128,512]{1,0:T(8,128)(2,1)S(1)}, u32[]{:S(2)}, u32[]{:S(2)}) %collective-permute-start.12) | collective-permute-done | bytes 131104 | tf_op jit(solution)/shard_map/ppermute | solution.py:22
  126.6 6.0 %collective-permute-done.11 = bf16[128,512]{1,0:T(8,128)(2,1)S(1)} collective-permute-done((bf16[128,512]{1,0:T(8,128)(2,1)S(1)}, bf16[128,512]{1,0:T(8,128)(2,1)S(1)}, u32[]{:S(2)}, u32[]{:S(2)}) %collective-permute-start.11) | collective-permute-done | bytes 131104 | tf_op jit(solution)/shard_map/ppermute | solution.py:22
  132.8 23.3 %all_to_all.15 = bf16[32,8,128]{2,1,0:T(8,128)(2,1)S(1)} all-to-all(bf16[32,8,128]{2,1,0:T(8,128)(2,1)S(1)} %fusion), channel_id=1, replica_groups=mesh['prow'=16,'pcol'=32] {'pcol'}, dimensions={0} | all-to-all | bytes 131072 | tf_op jit(solution)/shard_map/all_to_all | solution.py:169
  156.9 3.9 %all-to-all-start.2 = ((bf16[32,8,128]{2,1,0:T(8,128)(2,1)}), bf16[32,8,128]{2,1,0:T(8,128)(2,1)S(1)}, u32[]{:S(2)}, u32[]{:S(2)}) async-start(bf16[32,8,128]{2,1,0:T(8,128)(2,1)} %broadcast_in_dim.89), calls=%async_computation.2 | async-start | bytes 131072 | tf_op jit(solution)/shard_map/all_to_all | solution.py:171
  161.6 0.8 copy.17
  162.4 11.1 %all-to-all-done.2 = bf16[32,8,128]{2,1,0:T(8,128)(2,1)S(1)} async-done(((bf16[32,8,128]{2,1,0:T(8,128)(2,1)}), bf16[32,8,128]{2,1,0:T(8,128)(2,1)S(1)}, u32[]{:S(2)}, u32[]{:S(2)}) %all-to-all-start.2) | async-done | bytes 65568 | tf_op jit(solution)/shard_map/all_to_all | solution.py:171
  173.4 0.8 convert_add_fusion.1
  (61 shorter events, 5.2 us)
Async XLA Ops:
  0.6 21.0 %collective-permute-start = (bf16[64,1024]{1,0:T(8,128)(2,1)}, bf16[64,1024]{1,0:T(8,128)(2,1)S(1)}, u32[]{:S(2)}, u32[]{:S(2)}) collective-permute-start(bf16[64,1024]{1,0:T(8,128)(2,1)} %bitcast.35), channel_id=1, source_target_pairs={{0,0},{1,1},{2,2},{3,3},{4,8},{5,9},{6,10},{7,11},{8,16},{9,17},{1... | collective-permute-start | bytes 393224 | tf_op jit(solution)/shard_map/ppermute | solution.py:22
  2.2 19.4 %collective-permute-start.1 = (bf16[64,1024]{1,0:T(8,128)(2,1)}, bf16[64,1024]{1,0:T(8,128)(2,1)S(1)}, u32[]{:S(2)}, u32[]{:S(2)}) collective-permute-start(bf16[64,1024]{1,0:T(8,128)(2,1)} %bitcast.36), channel_id=1, source_target_pairs={{0,4},{1,5},{2,6},{3,7},{4,12},{5,13},{6,14},{7,15},{8,20},{9,21},... | collective-permute-start | bytes 393224 | tf_op jit(solution)/shard_map/ppermute | solution.py:22
  11.7 30.4 %collective-permute-start.3 = (bf16[512,1024]{1,0:T(8,128)(2,1)}, bf16[512,1024]{1,0:T(8,128)(2,1)S(1)}, u32[]{:S(2)}, u32[]{:S(2)}) collective-permute-start(bf16[512,1024]{1,0:T(8,128)(2,1)} %near.3), channel_id=1, source_target_pairs={{0,8},{1,9},{2,10},{3,11},{4,12},{5,13},{6,14},{7,15},{8,0},{9,1},... | collective-permute-start | bytes 3145736 | tf_op jit(solution)/shard_map/ppermute | solution.py:22
  16.5 27.4 %collective-permute-start.4 = (bf16[512,1024]{1,0:T(8,128)(2,1)}, bf16[512,1024]{1,0:T(8,128)(2,1)S(1)}, u32[]{:S(2)}, u32[]{:S(2)}) collective-permute-start(bf16[512,1024]{1,0:T(8,128)(2,1)} %near.3), channel_id=1, source_target_pairs={{0,24},{1,25},{2,26},{3,27},{4,28},{5,29},{6,30},{7,31},{8,16},{9,... | collective-permute-start | bytes 3145736 | tf_op jit(solution)/shard_map/ppermute | solution.py:22
  19.0 0.7 copy-start.3
  19.1 0.7 copy-start.4
  20.6 0.7 copy-start.5
  21.6 6.1 %copy-start.1 = (bf16[1024,64]{0,1:T(8,128)(2,1)S(1)}, bf16[1024,64]{0,1:T(8,128)(2,1)}, u32[]{:S(2)}) copy-start(bf16[1024,64]{0,1:T(8,128)(2,1)} %param.7) | copy-start | bytes 393220
  21.6 20.4 %collective-permute-start.2 = (bf16[2,64,1024]{2,1,0:T(8,128)(2,1)S(1)}, bf16[2,64,1024]{2,1,0:T(8,128)(2,1)S(1)}, u32[]{:S(2)}, u32[]{:S(2)}) collective-permute-start(bf16[2,64,1024]{2,1,0:T(8,128)(2,1)S(1)} %get-tuple-element.41), channel_id=1, source_target_pairs={{0,2},{1,3},{2,0},{3,1},{4,6},{5,7},{6,4},{7,5},{8,10},{9,11},{10,... | collective-permute-start | bytes 786440 | tf_op jit(solution)/shard_map/ppermute | solution.py:22
  27.7 20.8 %collective-permute-start.8 = (bf16[64,512]{1,0:T(8,128)(2,1)S(1)}, bf16[64,512]{1,0:T(8,128)(2,1)S(1)}, u32[]{:S(2)}, u32[]{:S(2)}) collective-permute-start(bf16[64,512]{1,0:T(8,128)(2,1)S(1)} %get-tuple-element.44), channel_id=1, source_target_pairs={{0,0},{1,1},{2,32},{3,33},{4,64},{5,65},{6,96},{7,97},{8,128},{9,1... | collective-permute-start | bytes 196616 | tf_op jit(solution)/shard_map/ppermute | solution.py:22
  35.6 19.0 %collective-permute-start.9 = (bf16[64,512]{1,0:T(8,128)(2,1)S(1)}, bf16[64,512]{1,0:T(8,128)(2,1)S(1)}, u32[]{:S(2)}, u32[]{:S(2)}) collective-permute-start(bf16[64,512]{1,0:T(8,128)(2,1)S(1)} %get-tuple-element.45), channel_id=1, source_target_pairs={{0,1},{1,0},{2,33},{3,32},{4,65},{5,64},{6,97},{7,96},{8,129},{9,1... | collective-permute-start | bytes 196616 | tf_op jit(solution)/shard_map/ppermute | solution.py:22
  44.0 17.1 %collective-permute-start.5 = (bf16[2,2,64,1024]{3,2,0,1:T(8,128)(2,1)S(1)}, bf16[2,2,64,1024]{3,2,0,1:T(8,128)(2,1)S(1)}, u32[]{:S(2)}, u32[]{:S(2)}) collective-permute-start(bf16[2,2,64,1024]{3,2,0,1:T(8,128)(2,1)S(1)} %fusion.3), channel_id=1, source_target_pairs={{0,1},{1,0},{2,3},{3,2},{4,5},{5,4},{6,7},{7,6},{8,9},{9,8},{10,11... | collective-permute-start | bytes 1572872 | tf_op jit(solution)/shard_map/ppermute | solution.py:22
  54.6 12.1 %collective-permute-start.6 = (bf16[256,1024]{1,0:T(8,128)(2,1)S(1)}, bf16[256,1024]{1,0:T(8,128)(2,1)S(1)}, u32[]{:S(2)}, u32[]{:S(2)}) collective-permute-start(bf16[256,1024]{1,0:T(8,128)(2,1)S(1)} %slice.6), channel_id=1, source_target_pairs={{0,8},{1,9},{2,10},{3,11},{4,12},{5,13},{6,14},{7,15},{8,0},{9,1},... | collective-permute-start | bytes 1572872 | tf_op jit(solution)/shard_map/ppermute | solution.py:22
  58.1 15.9 %collective-permute-start.7 = (bf16[256,1024]{1,0:T(8,128)(2,1)S(1)}, bf16[256,1024]{1,0:T(8,128)(2,1)S(1)}, u32[]{:S(2)}, u32[]{:S(2)}) collective-permute-start(bf16[256,1024]{1,0:T(8,128)(2,1)S(1)} %slice.7), channel_id=1, source_target_pairs={{0,24},{1,25},{2,26},{3,27},{4,28},{5,29},{6,30},{7,31},{8,16},{9,... | collective-permute-start | bytes 1572872 | tf_op jit(solution)/shard_map/ppermute | solution.py:22
  61.4 12.5 %copy-start = (bf16[512,1024]{1,0:T(8,128)(2,1)S(1)}, bf16[512,1024]{1,0:T(8,128)(2,1)}, u32[]{:S(2)}) copy-start(bf16[512,1024]{1,0:T(8,128)(2,1)} %near.3) | copy-start | bytes 3145732
  75.2 4.6 %collective-permute-start.10 = (bf16[4,256,512]{2,1,0:T(8,128)(2,1)S(1)}, bf16[4,256,512]{2,1,0:T(8,128)(2,1)S(1)}, u32[]{:S(2)}, u32[]{:S(2)}) collective-permute-start(bf16[4,256,512]{2,1,0:T(8,128)(2,1)S(1)} %shard_map.77), channel_id=1, source_target_pairs={{0,32},{1,33},{2,34},{3,35},{4,36},{5,37},{6,38},{7,39},{8,40},{9,... | collective-permute-start | bytes 3145736 | tf_op jit(solution)/shard_map/ppermute | solution.py:22
  82.0 22.6 %all-to-all-start = ((bf16[4,256,512]{2,1,0:T(8,128)(2,1)}), bf16[4,256,512]{2,1,0:T(8,128)(2,1)S(1)}, u32[]{:S(2)}, u32[]{:S(2)}) async-start(bf16[4,256,512]{2,1,0:T(8,128)(2,1)} %shard_map.78), calls=%async_computation | async-start | bytes 2097152 | tf_op jit(solution)/shard_map/all_to_all | solution.py:157
  91.3 32.7 %collective-permute-start.13 = (bf16[128,512]{1,0:T(8,128)(2,1)S(1)}, bf16[128,512]{1,0:T(8,128)(2,1)S(1)}, u32[]{:S(2)}, u32[]{:S(2)}) collective-permute-start(bf16[128,512]{1,0:T(8,128)(2,1)S(1)} %fusion.11), channel_id=1, source_target_pairs={{0,32},{1,33},{2,34},{3,35},{4,36},{5,37},{6,38},{7,39},{8,40},{9,... | collective-permute-start | bytes 393224 | tf_op jit(solution)/shard_map/ppermute | solution.py:22
  104.9 21.7 %collective-permute-start.12 = (bf16[128,512]{1,0:T(8,128)(2,1)S(1)}, bf16[128,512]{1,0:T(8,128)(2,1)S(1)}, u32[]{:S(2)}, u32[]{:S(2)}) collective-permute-start(bf16[128,512]{1,0:T(8,128)(2,1)S(1)} %get-tuple-element.39), channel_id=1, source_target_pairs={{0,256},{1,257},{2,258},{3,259},{4,260},{5,261},{6,262},{7,263},{8... | collective-permute-start | bytes 393224 | tf_op jit(solution)/shard_map/ppermute | solution.py:22
  117.8 14.8 %collective-permute-start.11 = (bf16[128,512]{1,0:T(8,128)(2,1)S(1)}, bf16[128,512]{1,0:T(8,128)(2,1)S(1)}, u32[]{:S(2)}, u32[]{:S(2)}) collective-permute-start(bf16[128,512]{1,0:T(8,128)(2,1)S(1)} %get-tuple-element.38), channel_id=1, source_target_pairs={{0,0},{1,1},{2,2},{3,3},{4,4},{5,5},{6,6},{7,7},{8,64},{9,65},{10,... | collective-permute-start | bytes 393224 | tf_op jit(solution)/shard_map/ppermute | solution.py:22
  156.9 16.6 %all-to-all-start.2 = ((bf16[32,8,128]{2,1,0:T(8,128)(2,1)}), bf16[32,8,128]{2,1,0:T(8,128)(2,1)S(1)}, u32[]{:S(2)}, u32[]{:S(2)}) async-start(bf16[32,8,128]{2,1,0:T(8,128)(2,1)} %broadcast_in_dim.89), calls=%async_computation.2 | async-start | bytes 131072 | tf_op jit(solution)/shard_map/all_to_all | solution.py:171
  161.6 11.8 %copy-start.2 = (f32[256,128]{1,0:T(8,128)S(1)}, f32[256,128]{1,0:T(8,128)}, u32[]{:S(2)}) copy-start(f32[256,128]{1,0:T(8,128)} %param.8) | copy-start | bytes 393220
